TPU v7x, 256 devices: a whole 4x4x8 slice. The times are simulated.
256 devices in a mesh: row: 32 (over x, z), col: 8 (over y, core).
Axes of the slice: x: 4, y: 4, z: 8, core: 2. Of those that a mesh axis runs over, the one named last changes fastest.
Arguments:
- trailing: float32 [2, 12288, 12288], P(None, 'row', 'col'), may hold values from -6 to 6
- panel: bfloat16 [2, 12288, 512], P(None, ('row', 'col')), may hold values from -1.296875 to 1.296875
- diagonal: float32 [2, 512, 512], replicated, as said below
- pattern: int32 [96], replicated, may hold values 0 or 1
Outputs:
- updated: float32 [2, 12288, 12288], P(None, 'row', 'col')
- solved: float32 [2, 12288, 512], P(None, ('row', 'col'))
Inputs may be any that keep to these rules, and one draw needn't show every extreme that they name: symmetric; each diagonal entry exceeds the sum of magnitudes of the other entries of its row by 0.2 or more.
All inputs are finite; a program needn't handle non-finite values.
Results may differ from a plain program's by a relative error of at most 0.0003.
Values may be sent and summed in bfloat16 or wider, within the bound.
A program may use at most 128 MiB of HBM per device.

v0:
```python
import jax
import jax.numpy as jnp
from jax import lax
from jax.sharding import PartitionSpec as P

BLK = 128


def per_device(trailing, panel, diagonal, pattern):
    count = panel.shape[1]
    width = panel.shape[2]
    n_row = lax.axis_size("row")
    n_col = lax.axis_size("col")
    first_row = (lax.axis_index("row") * n_col + lax.axis_index("col")) * count
    block_of = (first_row + jnp.arange(count, dtype=jnp.int32)) // BLK
    matches = block_of[:, None] == jnp.arange(pattern.shape[0], dtype=jnp.int32)[None, :]
    keep = jnp.sum(jnp.where(matches, pattern[None, :], 0), axis=1).astype(jnp.float32)
    factor = jnp.linalg.cholesky(diagonal)
    unit = jnp.eye(width, dtype=jnp.float32)
    inverse = jax.vmap(
        lambda lower_part: jax.scipy.linalg.solve_triangular(lower_part, unit, lower=True)
    )(factor)
    solved = jnp.einsum(
        "brk,bjk->brj", panel.astype(jnp.float32), inverse, precision=lax.Precision.HIGHEST
    )
    solved = solved * keep[None, :, None]
    rounded = solved.astype(jnp.bfloat16)
    row_panel = lax.all_gather(rounded, "col", axis=1, tiled=True)
    group_rows = row_panel.shape[1]
    ratio = n_row // n_col
    column_index = lax.axis_index("col")
    everything = lax.all_gather(row_panel, "row", axis=1, tiled=True)
    column_panel = lax.dynamic_slice_in_dim(
        everything, column_index * ratio * group_rows, ratio * group_rows, 1
    )
    update = jnp.einsum("bik,bjk->bij", row_panel, column_panel, preferred_element_type=jnp.float32)
    return (trailing - update, solved)


def solution(mesh):
    return jax.shard_map(
        per_device,
        mesh=mesh,
        in_specs=(P(None, "row", "col"), P(None, ("row", "col"), None), P(), P()),
        out_specs=(P(None, "row", "col"), P(None, ("row", "col"), None)),
        check_vma=False,
    )
```

profile of v0, /device:TPU:1, one launch (start us, length us, event | category | flops | bytes accessed | tf_op | source)
XLA Modules:
  0.0 497.4 jit_solution(676550873883435128)
XLA Ops:
  7.5 1.0 select_reduce_fusion.4
  8.6 1.0 fusion.53
  9.6 1.8 copy.17
  11.4 2.1 fusion.9
  13.5 1.3 copy-done.2
  14.8 23.5 %custom-call.35 = f32[2,128,128]{2,1,0:T(8,128)S(1)} custom-call(f32[2,128,128]{2,1,0:T(8,128)S(1)} %cholesky.274), custom_call_target="Cholesky" | custom-call | tf_op jit(solution)/shard_map/jit(cholesky)/cholesky | solution.py:18
  38.3 19.7 %custom-call.36 = f32[2,1,128,128]{2,3,1,0:T(8,128)S(1)} custom-call(f32[2,1,128,128]{3,2,1,0:T(8,128)S(1)} %select_bitcast_fusion.2), custom_call_target="InvertDiagBlocksLowerTriangular" | custom-call | tf_op jit(solution)/shard_map/jit(cholesky)/cholesky | solution.py:18
  58.3 1.5 constant_dynamic-update-slice_fusion.3
  59.8 1.5 convolution_subtract_fusion.3
  61.3 23.5 %custom-call.37 = f32[2,128,128]{2,1,0:T(8,128)S(1)} custom-call(f32[2,128,128]{2,1,0:T(8,128)S(1)} %cholesky.278), custom_call_target="Cholesky" | custom-call | tf_op jit(solution)/shard_map/jit(cholesky)/cholesky | solution.py:18
  84.8 20.1 %custom-call.38 = f32[2,1,128,128]{2,3,1,0:T(8,128)S(1)} custom-call(f32[2,1,128,128]{3,2,1,0:T(8,128)S(1)} %get-tuple-element.31), custom_call_target="InvertDiagBlocksLowerTriangular" | custom-call | tf_op jit(solution)/shard_map/jit(cholesky)/cholesky | solution.py:18
  105.3 1.6 convolution_subtract_fusion.4
  106.9 23.5 %custom-call.39 = f32[2,128,128]{2,1,0:T(8,128)S(1)} custom-call(f32[2,128,128]{2,1,0:T(8,128)S(1)} %cholesky.283), custom_call_target="Cholesky" | custom-call | tf_op jit(solution)/shard_map/jit(cholesky)/cholesky | solution.py:18
  130.4 19.7 %custom-call.40 = f32[2,1,128,128]{2,3,1,0:T(8,128)S(1)} custom-call(f32[2,1,128,128]{3,2,1,0:T(8,128)S(1)} %get-tuple-element.29), custom_call_target="InvertDiagBlocksLowerTriangular" | custom-call | tf_op jit(solution)/shard_map/jit(cholesky)/cholesky | solution.py:18
  150.4 1.5 convolution_subtract_fusion.5
  151.9 23.6 %custom-call.41 = f32[2,128,128]{2,1,0:T(8,128)S(1)} custom-call(f32[2,128,128]{2,1,0:T(8,128)S(1)} %convolution_subtract_fusion.5), custom_call_target="Cholesky" | custom-call | tf_op jit(solution)/shard_map/jit(cholesky)/cholesky | solution.py:18
  175.9 1.7 select_select_fusion
  177.6 14.5 %while.1 = (s32[]{:T(128)}, f32[2,512,512]{2,1,0:T(8,128)}, s32[4,2]{0,1:T(2,128)S(1)}, f32[4,2,128,128]{3,2,0,1:T(8,128)}, s32[]{:T(128)}) while((s32[]{:T(128)}, f32[2,512,512]{2,1,0:T(8,128)}, s32[4,2]{0,1:T(2,128)S(1)}, f32[4,2,128,128]{3,2,0,1:T(8,128)}, s32[]{:T(128)}) %tuple.36), condition=%wide.while_cond, body=%wide.while_body.sunk | while | flops 2 | bytes 263277 | solution.py:21
  178.3 3.0 bitcast_dynamic-update-slice_fusion.2
  181.9 3.0 bitcast_dynamic-update-slice_fusion.2
  185.5 3.0 bitcast_dynamic-update-slice_fusion.2
  189.2 2.9 bitcast_dynamic-update-slice_fusion.2
  192.1 79.7 %custom-call.42 = f32[2,4,128,128]{2,3,1,0:T(8,128)S(1)} custom-call(f32[2,4,128,128]{3,2,1,0:T(8,128)} %bitcast.61), custom_call_target="InvertDiagBlocksLowerTriangular" | custom-call | tf_op jit(solution)/shard_map/vmap(jit(_solve_triangular))/triangular_solve | solution.py:21
  272.4 1.5 convolution_subtract_fusion.2
  273.9 0.6 fusion.42
  274.6 1.7 convolution_subtract_fusion.1
  276.9 2.1 fusion.16
  279.0 0.6 fusion.39
  279.7 1.8 fusion.54
  281.5 17.5 %all_gather.6 = bf16[2,384,512]{2,1,0:T(8,128)(2,1)} all-gather(bf16[2,48,512]{2,1,0:T(8,128)(2,1)S(1)} %get-tuple-element.35), channel_id=1, replica_groups=mesh['row'=32,'col'=8] {'col'}, dimensions={1}, use_global_device_ids=true | all-gather | bytes 884736 | tf_op jit(solution)/shard_map/all_gather | solution.py:28
  299.1 184.1 %all-gather.2.cloned.1.call-done = bf16[2,12288,512]{2,1,0:T(8,128)(2,1)} async-done(((bf16[2,384,512]{2,1,0:T(8,128)(2,1)}), bf16[2,12288,512]{2,1,0:T(8,128)(2,1)}) %all-gather.2.cloned.1.call-update) | async-done | bytes 25165840 | tf_op jit(solution)/shard_map/all_gather | solution.py:32
  483.2 7.2 %convolution_subtract_fusion = f32[2,384,1536]{2,1,0:T(8,128)} fusion(f32[2,384,1536]{2,1,0:T(8,128)} %param.4, bf16[2,384,512]{2,1,0:T(8,128)(2,1)} %all_gather.6, bf16[2,12288,512]{2,1,0:T(8,128)(2,1)} %all-gather.2.cloned.1.call-done, s32[]{:T(128)S(6)} %select_n.23), kind=kOutput, calls=%fused_computation.2 | convolution fusion | flops 1209139200 | bytes 13369348 | tf_op jit(solution)/shard_map/bik,bjk->bij/dot_general | solution.py:36
  (47 shorter events, 5.6 us)
Async XLA Ops:
  7.2 272.5 %copy-start = (bf16[2,48,512]{2,1,0:T(8,128)(2,1)S(1)}, bf16[2,48,512]{2,1,0:T(8,128)(2,1)}, u32[]{:S(2)}) copy-start(bf16[2,48,512]{2,1,0:T(8,128)(2,1)} %param.5) | copy-start | bytes 294916
  7.2 2.4 copy-start.1
  7.2 476.0 %all-gather.2.cloned.1.call-start = ((), (), s32[]{:S(2)}) async-start(), calls=%async_computation | async-start | bytes 25952256 | tf_op jit(solution)/shard_map/all_gather | solution.py:32
  13.5 1.3 copy-start.2
  175.9 95.9 %copy-start.3 = (f32[128,512]{1,0:T(8,128)S(1)}, f32[128,512]{1,0:T(8,128)}, u32[]{:S(2)}) copy-start(f32[128,512]{1,0:T(8,128)} %get-tuple-element.27) | copy-start | bytes 786436
  177.6 94.8 %copy-start.4 = (f32[128,512]{1,0:T(8,128)S(1)}, f32[128,512]{1,0:T(8,128)}, u32[]{:S(2)}) copy-start(f32[128,512]{1,0:T(8,128)} %get-tuple-element.26) | copy-start | bytes 786436
  192.1 82.5 %copy-start.6 = (f32[128,512]{1,0:T(8,128)S(1)}, f32[128,512]{1,0:T(8,128)}, u32[]{:S(2)}) copy-start(f32[128,512]{1,0:T(8,128)} %get-tuple-element.25) | copy-start | bytes 786436
  273.9 3.0 copy-start.5
Sparse Core Ops, SparseCore 0:
  299.2 183.9 all-gather.1
where the time goes:
time: 507 us; the launch traced here: 497 us
  other arithmetic  239 us (47%)
  waiting for transfers between devices  184 us (36%)
  matrix products  23.5 us (5%)
  local copies, waits for them, and re-layouts  18.9 us (4%)
  blocking collectives  17.5 us (3%)
  between operations  14.6 us (3%)
    all_gather x1, waiting for transfers between devices, per_device(): everything = lax.all_gather(row_panel, 'row', axis=1, tiled=True)  184 us
    another operation x16, other arithmetic, per_device(): factor = jnp.linalg.cholesky(diagonal)  154 us
    another operation x4, other arithmetic, per_device(): jax.scipy.linalg.solve_triangular(lower_part, unit, lower=True)  81.5 us
    all_gather x1, blocking collectives, per_device(): row_panel = lax.all_gather(rounded, 'col', axis=1, tiled=True)  17.5 us
    another operation x12, local copies, waits for them, and re-layouts  14.5 us
  transfers between devices with their start and end apart: 1, of which 1 were waited for; matrix products, arithmetic and copies ran while one was open for 0% of the time, Pallas kernels for 0%

commit v1 on v0

v1 whole, which is shorter than its diff:
```python
import jax, jax.numpy as jnp
from jax import lax
from jax.experimental import pallas as pl
from jax.experimental.pallas import tpu as pltpu
from jax.sharding import PartitionSpec as P

BLK = 128
F32=jnp.float32
HI=lax.Precision.HIGHEST

def dot(a,b,ca,cb):
    return lax.dot_general(a,b,(((ca,),(cb,)),((),())),precision=HI,preferred_element_type=F32)

def bc(x,k):
    return jnp.broadcast_to(x[k:k+1,:],(8,128))

def base(X):
    lane = lax.broadcasted_iota(jnp.int32,(8,128),1)
    sub = lax.broadcasted_iota(jnp.int32,(8,128),0)
    half = jnp.where(lane<64,0,64)
    l64 = lane-half
    E=[jnp.where(l64==sub+8*g,1.0,0.0).astype(F32) for g in range(8)]
    X=list(X)
    out=[]
    for p in range(8):
        T={}
        for g in range(p,8):
            T[g]=[jnp.take_along_axis(X[g],half+(8*p+c),axis=1,mode="promise_in_bounds") for c in range(8)]
        dv=T[p][0]
        for k in range(8):
            d=bc(T[p][k],k)
            dv=jnp.where(sub==k,d,dv)
            r=1.0/d
            pe=bc(E[p],k)
            px=bc(X[p],k)
            tr={c:bc(T[p][c],k) for c in range(k+1,8)}
            for g in range(p,8):
                m=T[g][k]*r
                if g==p:
                    if k==7: continue
                    m=jnp.where(sub>k,m,0.0)
                for c in range(k+1,8):
                    T[g][c]=T[g][c]-m*tr[c]
                if p<7: X[g]=X[g]-m*px
                E[g]=E[g]-m*pe
        out.append(E[p]*lax.rsqrt(dv))
    return out

def chol_kernel(d_ref, hi_ref, mid_ref, lo_ref, W):
    for b in range(2):
        W[b]=d_ref[b]
    lane=lax.broadcasted_iota(jnp.int32,(8,128),1)
    lane512=lax.broadcasted_iota(jnp.int32,(64,512),1)
    def step(t, carry):
        o=pl.multiple_of(t*128,128)
        for s in range(2):
            os=pl.multiple_of(o+64*s,64)
            X=[]
            for g in range(8):
                a0=W[0,pl.ds(pl.multiple_of(os+8*g,8),8),pl.ds(o,128)]
                a1=W[1,pl.ds(pl.multiple_of(os+8*g,8),8),pl.ds(o,128)]
                if s==0: X.append(jnp.where(lane<64,a0,pltpu.roll(a1,64,1)))
                else: X.append(jnp.where(lane<64,pltpu.roll(a0,64,1),a1))
            Y=jnp.concatenate(base(X),axis=0)
            for b in range(2):
                Yb=Y[:,64*b:64*b+64]
                V=W[b,pl.ds(os,64),:]
                Vn=dot(Yb,V,1,0)
                Yt=jnp.concatenate([Yb,Yb]*4,axis=1)
                injj=(lane512>=os)&(lane512<os+64)
                Vn=jnp.where(injj,Yt,Vn)
                W[b,pl.ds(os,64),:]=Vn
                def chunk(i,c):
                    ro=pl.multiple_of(i*128,128)
                    L=W[b,pl.ds(ro,128),pl.ds(o,128)][:,64*s:64*s+64]
                    Ln=dot(L,Yb,1,1)
                    row=lax.broadcasted_iota(jnp.int32,(128,64),0)+ro
                    Ln=jnp.where(row>=os+64,Ln,0.0)
                    rr=lax.broadcasted_iota(jnp.int32,(128,512),0)+ro
                    ll=lax.broadcasted_iota(jnp.int32,(128,512),1)
                    old=W[b,pl.ds(ro,128),:]
                    old=jnp.where((rr>=os+64)&(ll>=os)&(ll<os+64),0.0,old)
                    W[b,pl.ds(ro,128),:]=old-dot(Ln,Vn,1,0)
                    return c
                lax.fori_loop(t if s==0 else t+1,4,chunk,0)
        return carry
    lax.fori_loop(0,4,step,0)
    for b in range(2):
        r=lax.broadcasted_iota(jnp.int32,(512,512),0)
        l=lax.broadcasted_iota(jnp.int32,(512,512),1)
        y=jnp.where(r>=l,W[b],0.0)
        hi=y.astype(jnp.bfloat16)
        y=y-hi.astype(F32)
        mid=y.astype(jnp.bfloat16)
        lo=(y-mid.astype(F32)).astype(jnp.bfloat16)
        hi_ref[b]=hi
        mid_ref[b]=mid
        lo_ref[b]=lo

def cholinv(d):
    return pl.pallas_call(chol_kernel,out_shape=[jax.ShapeDtypeStruct(d.shape,jnp.bfloat16)]*3,name="cholinv",
      scratch_shapes=[pltpu.VMEM(d.shape,F32)],
      cost_estimate=pl.CostEstimate(flops=20*10**9,bytes_accessed=5*10**6,transcendentals=0),
      compiler_params=pltpu.CompilerParams(vmem_limit_bytes=48<<20))(d)


def solve_rows(p, y_refs, b):
    half = p.shape[1] // 2
    parts = []
    for lo, depth in ((0, half), (half, 2 * half)):
        acc = None
        for y in y_refs:
            term = lax.dot_general(
                p[:, :depth],
                y[b, lo : lo + half, :depth],
                (((1,), (1,)), ((), ())),
                preferred_element_type=F32,
            )
            acc = term if acc is None else acc + term
        parts.append(acc)
    return jnp.concatenate(parts, axis=1)


def keep_rows(x, pat_ref, first_block):
    blocks = [
        x[i * BLK : (i + 1) * BLK] * pat_ref[first_block + i].astype(F32)
        for i in range(x.shape[0] // BLK)
    ]
    return jnp.concatenate(blocks, axis=0)


def update_kernel(pat_ref, own_ref, row_ref, col_ref, hi_ref, mid_ref, lo_ref, trail_ref, out_ref, solved_ref, rows):
    b = pl.program_id(0)
    tile = pl.program_id(1)
    row, col = lax.axis_index("row"), lax.axis_index("col")
    ys = (hi_ref, mid_ref, lo_ref)

    @pl.when(tile == 0)
    def _():
        r = solve_rows(row_ref[0], ys, b)
        rows[...] = keep_rows(r, pat_ref, row * 3).astype(jnp.bfloat16)
        own = solve_rows(own_ref[0], ys, b)
        first = (row * 8 + col) * 48
        low = first // BLK
        high = (first + 47) // BLK
        at = first + lax.broadcasted_iota(jnp.int32, own.shape, 0)
        keep = jnp.where(at < high * BLK, pat_ref[low], pat_ref[high]).astype(F32)
        solved_ref[0] = own * keep

    c = solve_rows(col_ref[0], ys, b)
    per = col_ref.shape[1] // BLK
    c = keep_rows(c, pat_ref, col * 12 + tile * per).astype(jnp.bfloat16)
    out_ref[0] = trail_ref[0] - lax.dot_general(
        rows[...], c, (((1,), (1,)), ((), ())), preferred_element_type=F32
    )


def update(pattern, own, rowp, colp, ys, trailing):
    nb, m, n = trailing.shape
    width = 512
    k = own.shape[2]
    whole = pl.BlockSpec((nb, k, k), lambda b, t: (0, 0, 0))
    return pl.pallas_call(
        update_kernel,
        grid=(nb, n // width),
        in_specs=[
            pl.BlockSpec(memory_space=pltpu.SMEM),
            pl.BlockSpec((1, own.shape[1], k), lambda b, t: (b, 0, 0)),
            pl.BlockSpec((1, m, k), lambda b, t: (b, 0, 0)),
            pl.BlockSpec((1, width, k), lambda b, t: (b, t, 0)),
            whole,
            whole,
            whole,
            pl.BlockSpec((1, m, width), lambda b, t: (b, 0, t)),
        ],
        out_specs=[
            pl.BlockSpec((1, m, width), lambda b, t: (b, 0, t)),
            pl.BlockSpec((1, own.shape[1], k), lambda b, t: (b, 0, 0)),
        ],
        out_shape=[
            jax.ShapeDtypeStruct(trailing.shape, F32),
            jax.ShapeDtypeStruct(own.shape, F32),
        ],
        scratch_shapes=[pltpu.VMEM((m, k), jnp.bfloat16)],
        compiler_params=pltpu.CompilerParams(vmem_limit_bytes=48 << 20),
        cost_estimate=pl.CostEstimate(flops=6 * 10**9, bytes_accessed=16 * 10**6, transcendentals=0),
        name="solve_update",
    )(pattern, own, rowp, colp, *ys, trailing)


def per_device(trailing, panel, diagonal, pattern):
    n_row = lax.axis_size("row")
    n_col = lax.axis_size("col")
    ratio = n_row // n_col
    perm = [
        (r * n_col + c, ((r % ratio) * n_col + c) * n_col + r // ratio)
        for r in range(n_row)
        for c in range(n_col)
    ]
    moved = lax.ppermute(panel, ("row", "col"), perm)
    rowp = lax.all_gather(panel, "col", axis=1, tiled=True)
    colp = lax.all_gather(moved, "row", axis=1, tiled=True)
    ys = cholinv(diagonal)
    return tuple(update(pattern, panel, rowp, colp, ys, trailing))


def solution(mesh):
    return jax.shard_map(
        per_device,
        mesh=mesh,
        in_specs=(P(None, "row", "col"), P(None, ("row", "col"), None), P(), P()),
        out_specs=(P(None, "row", "col"), P(None, ("row", "col"), None)),
        check_vma=False,
    )
```

time: 507 us -> 127 us (0.25)
  the two profiles are of different devices: /device:TPU:1 before, /device:TPU:2 now
where the time goes in v1:
time: 127 us; the launch traced here: 126 us
  Pallas kernels  53.1 us (42%)
  waiting for transfers between devices  28.8 us (23%)
  blocking collectives  21.7 us (17%)
  between operations  14.1 us (11%)
  local copies, waits for them, and re-layouts  4.46 us (4%)
  starting transfers between devices  3.5 us (3%)
    pallas_call x1, Pallas kernels, cholinv(): pl.pallas_call(chol_kernel, out_shape=[jax.ShapeDtypeStruct(d.shape, jnp....  40.2 us
    all_gather x1, waiting for transfers between devices, per_device(): colp = lax.all_gather(moved, 'row', axis=1, tiled=True)  24.6 us
    all_gather x1, blocking collectives, per_device(): rowp = lax.all_gather(panel, 'col', axis=1, tiled=True)  21.7 us
    pallas_call x1, Pallas kernels, update(): pl.pallas_call(update_kernel, grid=(nb, n // width), in_specs=[pl.BlockSp...  12.9 us
    unnamed x12, local copies, waits for them, and re-layouts  4.46 us
    ppermute x1, waiting for transfers between devices, per_device(): moved = lax.ppermute(panel, ('row', 'col'), perm)  4.16 us
    ppermute x1, starting transfers between devices, per_device(): moved = lax.ppermute(panel, ('row', 'col'), perm)  3.46 us
  transfers between devices with their start and end apart: 2, of which 2 were waited for; matrix products, arithmetic and copies ran while one was open for 0% of the time, Pallas kernels for 32%

profile of v1, /device:TPU:2, one launch (start us, length us, event | category | flops | bytes accessed | tf_op | source)
XLA Modules:
  0.0 125.6 jit_solution(14017637694209140308)
XLA Ops:
  7.2 0.0 all-gather.2.cloned.1.call-start
  7.2 3.5 %collective-permute-start = (bf16[2,48,512]{2,1,0:T(8,128)(2,1)}, bf16[2,48,512]{2,1,0:T(8,128)(2,1)S(1)}, u32[]{:S(2)}, u32[]{:S(2)}) collective-permute-start(bf16[2,48,512]{2,1,0:T(8,128)(2,1)} %own_ref.1), channel_id=1, source_target_pairs={{0,0},{1,8},{2,16},{3,24},{4,32},{5,40},{6,48},{7,56},{8,64},{9,72... | collective-permute-start | bytes 294920 | tf_op jit(solution)/shard_map/ppermute | solution.py:200
  10.7 4.2 %collective-permute-done = bf16[2,48,512]{2,1,0:T(8,128)(2,1)S(1)} collective-permute-done((bf16[2,48,512]{2,1,0:T(8,128)(2,1)}, bf16[2,48,512]{2,1,0:T(8,128)(2,1)S(1)}, u32[]{:S(2)}, u32[]{:S(2)}) %collective-permute-start) | collective-permute-done | bytes 98336 | tf_op jit(solution)/shard_map/ppermute | solution.py:200
  14.8 0.0 copy-start.5
  14.8 0.6 copy-done.5
  15.5 0.0 all-gather.2.cloned.1.call-update
  15.5 21.7 %all_gather.6.row_ref = bf16[2,384,512]{2,1,0:T(8,128)(2,1)S(1)} all-gather(bf16[2,48,512]{2,1,0:T(8,128)(2,1)} %own_ref.1), channel_id=1, replica_groups=mesh['row'=32,'col'=8] {'col'}, dimensions={1}, use_global_device_ids=true | all-gather | bytes 884736 | tf_op jit(solution)/shard_map/all_gather | solution.py:201
  37.2 0.0 copy-start.1
  37.2 1.6 %copy-done.1 = f32[2,512,512]{2,1,0:T(8,128)S(1)} copy-done((f32[2,512,512]{2,1,0:T(8,128)S(1)}, f32[2,512,512]{2,1,0:T(8,128)}, u32[]{:S(2)}) %copy-start.1) | copy-done | bytes 2097176
  38.8 0.0 copy-start
  38.8 0.0 copy-start.2
  38.8 40.2 %cholinv.1 = (bf16[2,512,512]{2,1,0:T(8,128)(2,1)S(1)}, bf16[2,512,512]{2,1,0:T(8,128)(2,1)S(1)}, bf16[2,512,512]{2,1,0:T(8,128)(2,1)S(1)}) custom-call(f32[2,512,512]{2,1,0:T(8,128)S(1)} %copy-done.1), custom_call_target="tpu_custom_call" | custom-call | flops 20000000000 | bytes 5000000 | tf_op jit(solution)/shard_map/cholinv/pallas_call | solution.py:101
  79.0 0.0 copy-start.3
  79.0 1.0 copy-done.3
  80.0 24.6 %all-gather.2.cloned.1.call-done.col_ref = bf16[2,1536,512]{2,1,0:T(8,128)(2,1)} async-done(((bf16[2,48,512]{2,1,0:T(8,128)(2,1)}), bf16[2,1536,512]{2,1,0:T(8,128)(2,1)}) %all-gather.2.cloned.1.call-update) | async-done | bytes 3145744 | tf_op jit(solution)/shard_map/all_gather | solution.py:202
  104.6 0.0 copy-done
  104.6 0.0 copy-done.2
  104.6 0.0 copy-start.4
  104.6 1.2 copy-done.4
  105.8 12.9 %solve_update.1 = (f32[2,384,1536]{2,1,0:T(8,128)}, f32[2,48,512]{2,1,0:T(8,128)}) custom-call(s32[96]{0:T(128)S(1)} %copy-done.2, bf16[2,48,512]{2,1,0:T(8,128)(2,1)S(1)} %copy-done, bf16[2,384,512]{2,1,0:T(8,128)(2,1)S(1)} %all_gather.6.row_ref, bf16[2,1536,512]{2,1,0:T(8,128)(2,1)} %all-gather.2.cloned.1.call-done.col_ref, ...), custom_call_target="tpu_custom_call" | custom-call | flops 6000000000 | bytes 16000000 | tf_op jit(solution)/shard_map/solve_update/pallas_call | solution.py:163
Async XLA Ops:
  7.2 97.5 %all-gather.2.cloned.1.call-start = ((), (), s32[]{:S(2)}) async-start(), calls=%async_computation | async-start | bytes 3244032 | tf_op jit(solution)/shard_map/all_gather | solution.py:202
  7.2 7.6 %collective-permute-start = (bf16[2,48,512]{2,1,0:T(8,128)(2,1)}, bf16[2,48,512]{2,1,0:T(8,128)(2,1)S(1)}, u32[]{:S(2)}, u32[]{:S(2)}) collective-permute-start(bf16[2,48,512]{2,1,0:T(8,128)(2,1)} %own_ref.1), channel_id=1, source_target_pairs={{0,0},{1,8},{2,16},{3,24},{4,32},{5,40},{6,48},{7,56},{8,64},{9,72... | collective-permute-start | bytes 294920 | tf_op jit(solution)/shard_map/ppermute | solution.py:200
  14.8 0.6 copy-start.5
  37.2 1.6 %copy-start.1 = (f32[2,512,512]{2,1,0:T(8,128)S(1)}, f32[2,512,512]{2,1,0:T(8,128)}, u32[]{:S(2)}) copy-start(f32[2,512,512]{2,1,0:T(8,128)} %d_ref.1) | copy-start | bytes 6291460
  38.8 65.8 %copy-start = (bf16[2,48,512]{2,1,0:T(8,128)(2,1)S(1)}, bf16[2,48,512]{2,1,0:T(8,128)(2,1)}, u32[]{:S(2)}) copy-start(bf16[2,48,512]{2,1,0:T(8,128)(2,1)} %own_ref.1) | copy-start | bytes 294916
  38.8 65.8 %copy-start.2 = (s32[96]{0:T(128)S(1)}, s32[96]{0:T(128)}, u32[]{:S(2)}) copy-start(s32[96]{0:T(128)} %pat_ref.1) | copy-start | bytes 1156
  79.0 1.0 copy-start.3
  104.6 1.2 copy-start.4
Sparse Core Ops, SparseCore 0:
  15.6 88.9 all-gather.1

commit v2 on v1

v2 whole, which is shorter than its diff:
```python
import functools

import jax
import jax.numpy as jnp
from jax import lax
from jax.experimental import pallas as pl
from jax.experimental.pallas import tpu as pltpu
from jax.sharding import PartitionSpec as P

BLK = 128
F32 = jnp.float32
BF = jnp.bfloat16
HIGHEST = lax.Precision.HIGHEST
MESH = pl.DeviceIdType.MESH
NX, NZ, NC = 4, 8, 8

PLAN = {
    11: [('A', 0, 0), ('B', 0, 0)],
    19: [('A', 1, 0), ('A', -1, 0), ('A', 0, 1), ('A', 0, -1)],
    21: [('B', 1, 0), ('B', -1, 0), ('B', 0, 1), ('B', 0, -1)],
    25: [('A', 2, 0)],
    30: [('A', 1, 1), ('A', -1, 1), ('A', 0, 2), ('A', 1, -1), ('A', -1, -1), ('A', 0, -2)],
    33: [('B', -1, 1), ('B', -1, -1), ('A', 2, 1), ('A', 2, -1)],
    34: [('B', 0, 2), ('B', 0, -2)],
    36: [('B', 2, 0), ('B', 1, 1), ('B', 1, -1)],
    41: [('A', 1, 2), ('A', -1, 2), ('A', 0, 3), ('A', 1, -2), ('A', -1, -2), ('A', 0, -3)],
    43: [('A', 2, 2), ('A', 2, -2)],
    45: [('B', 0, 3), ('B', 0, -3)],
    46: [('B', 1, 2), ('B', 1, -2)],
    50: [('A', 1, -3), ('A', -1, -3)],
    51: [('A', 2, -3), ('B', 2, 1), ('B', 2, -1)],
    53: [('A', 1, 3), ('A', -1, 3), ('A', 0, 4), ('B', -1, 2), ('B', -1, -2)],
    54: [('A', 2, 3)],
    56: [('B', 0, 4)],
    57: [('A', -1, 4)],
    58: [('A', 2, 4)],
    59: [('B', -1, 3), ('B', -1, -3), ('A', 1, 4)],
    63: [('B', 1, 3), ('B', 1, -3)],
    64: [('B', 2, 2), ('B', 2, -2), ('B', -1, 4), ('B', 1, 4), ('B', 2, 3), ('B', 2, -3), ('B', 2, 4)],
}
PART = {"A": (0, 16), "B": (16, 32)}


def onward(part, dx, dz):
    out = []
    along_x = part == "B" or dz == 0
    along_z = part == "A" or dx == 0
    if along_x:
        if dx == 0:
            out += [("x", 1, 1, dz), ("x", -1, -1, dz)]
        elif dx == 1 and (part == "A" or dz % 2 == 0):
            out += [("x", 1, 2, dz)]
        elif dx == -1 and part == "B" and dz % 2 == 1:
            out += [("x", -1, 2, dz)]
    if along_z:
        if dz == 0:
            out += [("z", 1, dx, 1), ("z", -1, dx, -1)]
        elif 0 < dz < 3 or (dz == 3 and (part == "B" or dx in (0, 1))):
            out += [("z", 1, dx, dz + 1)]
        elif -3 < dz < 0 or (dz == -3 and part == "A" and dx in (2, -1)):
            out += [("z", -1, dx, dz - 1 if dz > -3 else 4)]
    return out


def rel(dx, dz):
    return (dx % NX) * NZ + dz % NZ


class Gather:
    def __init__(self, panel, cols, rows, first_sem, arrive_sem, send_sem, recv_sem, row_send, row_recv, own_sem):
        self.panel, self.cols, self.rows = panel, cols, rows
        self.first_sem, self.arrive_sem = first_sem, arrive_sem
        self.send_sem, self.recv_sem = send_sem, recv_sem
        self.row_send, self.row_recv, self.own_sem = row_send, row_recv, own_sem
        self.row, self.col = lax.axis_index("row"), lax.axis_index("col")
        self.x, self.z = self.row // NZ, self.row % NZ
        self.y, self.k = self.col // 2, self.col % 2
        x, y, z, k = self.x, self.y, self.z, self.k
        self.to_row = ((x + y) % NX) * NZ + (2 * (z % 4) + k + 6 + 4 * (z // 4)) % NZ
        self.to_col = 2 * x + z // 4
        self.to_slot = (z % 4) * NC + self.col
        u = (z + 10 - 4 * k) % NZ
        self.from_row = y * NZ + 4 * k + u // 2
        self.from_col = ((x + NX - y) % NX) * 2 + u % 2
        self.stays = (self.to_row == self.row) & (self.to_col == self.col)
        self.moves = jnp.logical_not(self.stays)
        self.home = self.slot(0, 0)
        self.sent = []

    def slot(self, dx, dz):
        xh = (self.x - dx + 2 * NX) % NX
        u = (self.z - dz + 2 * NZ + 10 - 4 * self.k) % NZ
        return (u // 2) * NC + ((xh + NX - self.y) % NX) * 2 + u % 2

    def neighbour(self, axis, step):
        if axis == "x":
            return (((self.x + step + NX) % NX) * NZ + self.z, self.col)
        return (self.x * NZ + (self.z + step + NZ) % NZ, self.col)

    def peer(self, i):
        return (self.row, (self.col + i) % NC)

    def barrier(self):
        sem = pltpu.get_barrier_semaphore()
        near = [self.neighbour(a, s) for a in "xz" for s in (1, -1)]
        near += [self.peer(i) for i in range(1, NC)]
        for d in near:
            pl.semaphore_signal(sem, inc=1, device_id=d, device_id_type=MESH)

        @pl.when(self.moves)
        def _():
            for d in ((self.to_row, self.to_col), (self.from_row, self.from_col)):
                pl.semaphore_signal(sem, inc=1, device_id=d, device_id_type=MESH)
            pl.semaphore_wait(sem, len(near) + 2)

        pl.when(self.stays)(lambda: pl.semaphore_wait(sem, len(near)))

    def first(self, slot):
        return pltpu.make_async_remote_copy(
            self.panel, self.cols.at[:, slot], self.first_sem, self.arrive_sem,
            device_id=(self.to_row, self.to_col), device_id_type=MESH,
        )

    def first_stays(self):
        return pltpu.make_async_copy(self.panel, self.cols.at[:, self.home], self.first_sem)

    def row_copy(self, i, col):
        return pltpu.make_async_remote_copy(
            self.panel, self.rows.at[:, col], self.row_send.at[i], self.row_recv.at[i],
            device_id=self.peer(i + 1), device_id_type=MESH,
        )

    def row_own(self):
        return pltpu.make_async_copy(self.panel, self.rows.at[:, self.col], self.own_sem)

    def start(self):
        pl.when(self.moves)(lambda: self.first(self.to_slot).start())
        pl.when(self.stays)(lambda: self.first_stays().start())
        for i in range(NC - 1):
            self.row_copy(i, self.col).start()
        self.row_own().start()

    def piece(self, part, slot):
        return self.cols.at[:, slot, pl.ds(*PART[part])]

    def move(self, part, slot, i, dx, dz, to):
        ref = self.piece(part, slot)
        return pltpu.make_async_remote_copy(
            ref, ref, self.send_sem.at[i], self.recv_sem.at[0 if part == "A" else 1, rel(dx, dz)],
            device_id=to, device_id_type=MESH,
        )

    def arrival(self, part, dx, dz):
        slot = self.slot(dx, dz)
        if (dx, dz) != (0, 0):
            self.move(part, slot, 0, dx, dz, self.neighbour("x", 1)).wait_recv()
        elif part == "A":
            pl.when(self.moves)(lambda: self.first(self.home).wait_recv())
            pl.when(self.stays)(lambda: self.first_stays().wait())
        for axis, step, ndx, ndz in onward(part, dx, dz):
            self.move(part, slot, len(self.sent), ndx, ndz, self.neighbour(axis, step)).start()
            self.sent.append(part)

    def point(self, h):
        for part, dx, dz in PLAN.get(h, ()):
            self.arrival(part, dx, dz)

    def wait_rows(self):
        for i in range(NC - 1):
            self.row_copy(i, (self.col + NC - 1 - i) % NC).wait_recv()
        self.row_own().wait()

    def drain(self):
        for i, part in enumerate(self.sent):
            self.move(part, self.home, i, 0, 0, self.neighbour("x", 1)).wait_send()
        pl.when(self.moves)(lambda: self.first(self.to_slot).wait_send())
        for i in range(NC - 1):
            self.row_copy(i, self.col).wait_send()


DMA = pltpu.SemaphoreType.DMA
GATHER_SEMS = [DMA, DMA, DMA((62,)), DMA((2, NX * NZ)), DMA((NC - 1,)), DMA((NC - 1,)), DMA]


def dot(a, b, ca, cb, precision=None):
    return lax.dot_general(
        a, b, (((ca,), (cb,)), ((), ())), precision=precision, preferred_element_type=F32
    )


def split3(x):
    hi = x.astype(BF)
    rest = x - hi.astype(F32)
    mid = rest.astype(BF)
    return hi, mid, (rest - mid.astype(F32)).astype(BF)


def stack6(x, axis, left):
    h, m, l = split3(x)
    return jnp.concatenate([h, h, m, h, l, m] if left else [h, m, h, l, h, m], axis=axis)


def spread(x, k):
    return jnp.broadcast_to(x[k : k + 1, :], (8, 128))


def base(x, point):
    lane = lax.broadcasted_iota(jnp.int32, (8, 128), 1)
    sub = lax.broadcasted_iota(jnp.int32, (8, 128), 0)
    half = jnp.where(lane < 64, 0, 64)
    x = list(x)
    e = [jnp.where(lane - half == sub + 8 * g, 1.0, 0.0).astype(F32) for g in range(8)]
    out = []
    for p in range(8):
        point(p)
        t = {
            g: [
                jnp.take_along_axis(x[g], half + (8 * p + c), axis=1, mode="promise_in_bounds")
                for c in range(8)
            ]
            for g in range(p, 8)
        }
        pivots = t[p][0]
        for k in range(8):
            d = spread(t[p][k], k)
            pivots = jnp.where(sub == k, d, pivots)
            r = 1.0 / d
            pe, px = spread(e[p], k), spread(x[p], k)
            top = {c: spread(t[p][c], k) for c in range(k + 1, 8)}
            for g in range(p, 8):
                if g == p and k == 7:
                    continue
                m = t[g][k] * r
                if g == p:
                    m = jnp.where(sub > k, m, 0.0)
                for c in range(k + 1, 8):
                    t[g][c] = t[g][c] - m * top[c]
                if p < 7:
                    x[g] = x[g] - m * px
                e[g] = e[g] - m * pe
        out.append(e[p] * lax.rsqrt(pivots))
    return jnp.concatenate(out, axis=0)


def factor(diag_ref, w, v, s6, point):
    for b in range(2):
        w[b] = diag_ref[b]
    lane = lax.broadcasted_iota(jnp.int32, (8, 128), 1)
    wide = lax.broadcasted_iota(jnp.int32, (64, 512), 1)
    wide2 = lax.broadcasted_iota(jnp.int32, (128, 512), 1)

    def step(t, carry):
        o = pl.multiple_of(t * 128, 128)
        for s in range(2):
            at = pl.multiple_of(o + 64 * s, 64)
            x = []
            for g in range(8):
                rows = pl.ds(pl.multiple_of(at + 8 * g, 8), 8)
                a, b = w[0, rows, pl.ds(o, 128)], w[1, rows, pl.ds(o, 128)]
                if s == 0:
                    x.append(jnp.where(lane < 64, a, pltpu.roll(b, 64, 1)))
                else:
                    x.append(jnp.where(lane < 64, pltpu.roll(a, 64, 1), b))
            y = base(x, functools.partial(point, t, s))
            here = (wide >= at) & (wide < at + 64)
            for b in range(2):
                yb = y[:, 64 * b : 64 * b + 64]
                new = dot(yb, w[b, pl.ds(at, 64), :], 1, 0, HIGHEST)
                new = jnp.where(here, jnp.concatenate([yb] * 8, axis=1), new)
                w[b, pl.ds(at, 64), :] = jnp.where(wide < at + 64, new, 0.0)
                if s == 0:
                    v[b, 0:64, :] = jnp.where((wide >= at + 64) & (wide < at + 128), 0.0, new)
                    below = w[b, pl.ds(at + 64, 64), pl.ds(o, 128)][:, 0:64]
                    lower = dot(below, yb, 1, 1, HIGHEST)
                    rest = jnp.where(here, 0.0, w[b, pl.ds(at + 64, 64), :])
                    w[b, pl.ds(at + 64, 64), :] = rest - dot(lower, new, 1, 0, HIGHEST)
                else:
                    v[b, 64:128, :] = new
        here = (wide2 >= o) & (wide2 < o + 128)

        @pl.when(t < 3)
        def _():
            for b in range(2):
                s6[b] = stack6(v[b], 0, False)

        def chunk(i, c):
            rows = pl.ds(pl.multiple_of(i * 128, 128), 128)
            for b in range(2):
                lower = v[b, :, rows].T
                rest = jnp.where(here, 0.0, w[b, rows, :])
                w[b, rows, :] = rest - dot(stack6(lower, 1, True), s6[b], 1, 0)
            return c

        lax.fori_loop(t + 1, 4, chunk, 0)
        return carry

    lax.fori_loop(0, 4, step, 0)


def gather_factor_kernel(panel, diag, hi, mid, lo, cols, rows, w, v, s6, *sems):
    gather = Gather(panel, cols, rows, *sems)
    gather.barrier()
    gather.start()

    def point(t, s, p):
        for i in range(4):
            h = (2 * i + s) * 8 + p
            if h in PLAN:
                pl.when(t == i)(functools.partial(gather.point, h))

    factor(diag, w, v, s6, point)
    for b in range(2):
        hi[b], mid[b], lo[b] = split3(w[b])
    gather.point(64)
    gather.wait_rows()
    gather.drain()


def gather_factor(panel, diagonal):
    nb, count, k = panel.shape
    vmem = pl.BlockSpec(memory_space=pltpu.VMEM)
    y = jax.ShapeDtypeStruct(diagonal.shape, BF)
    return pl.pallas_call(
        gather_factor_kernel,
        in_specs=[vmem] * 2,
        out_specs=[vmem] * 5,
        out_shape=[
            y, y, y,
            jax.ShapeDtypeStruct((nb, NX * NZ, count, k), BF),
            jax.ShapeDtypeStruct((nb, NC, count, k), BF),
        ],
        scratch_shapes=[
            pltpu.VMEM(diagonal.shape, F32),
            pltpu.VMEM((2, 128, 512), F32),
            pltpu.VMEM((2, 768, 512), BF),
        ] + GATHER_SEMS,
        compiler_params=pltpu.CompilerParams(
            collective_id=0, has_side_effects=True, vmem_limit_bytes=40 << 20
        ),
        cost_estimate=pl.CostEstimate(flops=10**10, bytes_accessed=10**7, transcendentals=0),
        name="gather_factor",
    )(panel, diagonal)


def solve_rows(p, y_refs, b):
    half = p.shape[1] // 2
    parts = []
    for lo, depth in ((0, half), (half, 2 * half)):
        acc = None
        for y in y_refs:
            term = lax.dot_general(
                p[:, :depth],
                y[b, lo : lo + half, :depth],
                (((1,), (1,)), ((), ())),
                preferred_element_type=F32,
            )
            acc = term if acc is None else acc + term
        parts.append(acc)
    return jnp.concatenate(parts, axis=1)


def keep_rows(x, pat_ref, first_block):
    blocks = [
        x[i * BLK : (i + 1) * BLK] * pat_ref[first_block + i].astype(F32)
        for i in range(x.shape[0] // BLK)
    ]
    return jnp.concatenate(blocks, axis=0)


def update_kernel(pat_ref, own_ref, row_ref, col_ref, hi_ref, mid_ref, lo_ref, trail_ref, out_ref, solved_ref, rows):
    b = pl.program_id(0)
    tile = pl.program_id(1)
    row, col = lax.axis_index("row"), lax.axis_index("col")
    ys = (hi_ref, mid_ref, lo_ref)

    @pl.when(tile == 0)
    def _():
        r = solve_rows(row_ref[0], ys, b)
        rows[...] = keep_rows(r, pat_ref, row * 3).astype(jnp.bfloat16)
        own = solve_rows(own_ref[0], ys, b)
        first = (row * 8 + col) * 48
        low = first // BLK
        high = (first + 47) // BLK
        at = first + lax.broadcasted_iota(jnp.int32, own.shape, 0)
        keep = jnp.where(at < high * BLK, pat_ref[low], pat_ref[high]).astype(F32)
        solved_ref[0] = own * keep

    c = solve_rows(col_ref[0], ys, b)
    per = col_ref.shape[1] // BLK
    c = keep_rows(c, pat_ref, col * 12 + tile * per).astype(jnp.bfloat16)
    out_ref[0] = trail_ref[0] - lax.dot_general(
        rows[...], c, (((1,), (1,)), ((), ())), preferred_element_type=F32
    )


def update(pattern, own, rowp, colp, ys, trailing):
    nb, m, n = trailing.shape
    width = 512
    k = own.shape[2]
    whole = pl.BlockSpec((nb, k, k), lambda b, t: (0, 0, 0))
    return pl.pallas_call(
        update_kernel,
        grid=(nb, n // width),
        in_specs=[
            pl.BlockSpec(memory_space=pltpu.SMEM),
            pl.BlockSpec((1, own.shape[1], k), lambda b, t: (b, 0, 0)),
            pl.BlockSpec((1, m, k), lambda b, t: (b, 0, 0)),
            pl.BlockSpec((1, width, k), lambda b, t: (b, t, 0)),
            whole,
            whole,
            whole,
            pl.BlockSpec((1, m, width), lambda b, t: (b, 0, t)),
        ],
        out_specs=[
            pl.BlockSpec((1, m, width), lambda b, t: (b, 0, t)),
            pl.BlockSpec((1, own.shape[1], k), lambda b, t: (b, 0, 0)),
        ],
        out_shape=[
            jax.ShapeDtypeStruct(trailing.shape, F32),
            jax.ShapeDtypeStruct(own.shape, F32),
        ],
        scratch_shapes=[pltpu.VMEM((m, k), jnp.bfloat16)],
        compiler_params=pltpu.CompilerParams(vmem_limit_bytes=48 << 20),
        cost_estimate=pl.CostEstimate(flops=6 * 10**9, bytes_accessed=16 * 10**6, transcendentals=0),
        name="solve_update",
    )(pattern, own, rowp, colp, *ys, trailing)


def per_device(trailing, panel, diagonal, pattern):
    hi, mid, lo, cols, rows = gather_factor(panel, diagonal)
    nb, _, _, k = cols.shape
    return tuple(update(pattern, panel, rows.reshape(nb, -1, k), cols.reshape(nb, -1, k), (hi, mid, lo), trailing))


def solution(mesh):
    return jax.shard_map(
        per_device,
        mesh=mesh,
        in_specs=(P(None, "row", "col"), P(None, ("row", "col"), None), P(), P()),
        out_specs=(P(None, "row", "col"), P(None, ("row", "col"), None)),
        check_vma=False,
    )
```

time: 127 us -> 64.4 us (0.51)
  waiting for transfers between devices: 28.8 us -> 0 us
  blocking collectives: 21.7 us -> 0 us
  between operations: 14.1 us -> 0.66 us
  Pallas kernels: 53.1 us -> 59.3 us
  starting transfers between devices: 3.5 us -> 0 us
    all_gather x1 -> x0, waiting for transfers between devices: 24.6 us -> none  [per_device(): colp = lax.all_gather(moved, 'row', axis=1, tiled=True)]
    all_gather x1 -> x0, blocking collectives: 21.7 us -> none  [per_device(): rowp = lax.all_gather(panel, 'col', axis=1, tiled=True)]
    pallas_call x1, Pallas kernels: 40.2 us -> 46.4 us  [gather_factor(): pl.pallas_call(gather_factor_kernel, in_specs=[vmem] * 2, out_specs=[vmem...]
    ppermute x1 -> x0, waiting for transfers between devices: 4.16 us -> none  [per_device(): moved = lax.ppermute(panel, ('row', 'col'), perm)]
    ppermute x1 -> x0, starting transfers between devices: 3.46 us -> none  [per_device(): moved = lax.ppermute(panel, ('row', 'col'), perm)]
    unnamed x12 -> x10, local copies, waits for them, and re-layouts: 4.46 us -> 4.13 us
  transfers between devices with their start and end apart: 2 -> 0, of which waited for: 2 -> 0; matrix products, arithmetic and copies ran while one was open for 0% -> 0% of each run, Pallas kernels for 32% -> 0%
where the time goes in v2:
time: 64.4 us; the launch traced here: 64.1 us
  Pallas kernels  59.3 us (92%)
  local copies, waits for them, and re-layouts  4.13 us (6%)
  between operations  0.66 us (1%)
    pallas_call x1, Pallas kernels, gather_factor(): pl.pallas_call(gather_factor_kernel, in_specs=[vmem] * 2, out_specs=[vmem...  46.4 us
    pallas_call x1, Pallas kernels, update(): pl.pallas_call(update_kernel, grid=(nb, n // width), in_specs=[pl.BlockSp...  12.9 us
    unnamed x10, local copies, waits for them, and re-layouts  4.13 us

profile of v2, /device:TPU:2, one launch (start us, length us, event | category | flops | bytes accessed | tf_op | source)
XLA Modules:
  0.0 64.1 jit_solution(1285944904573322976)
XLA Ops:
  0.6 0.0 copy-start
  0.6 1.6 %copy-done = f32[2,512,512]{2,1,0:T(8,128)S(1)} copy-done((f32[2,512,512]{2,1,0:T(8,128)S(1)}, f32[2,512,512]{2,1,0:T(8,128)}, u32[]{:S(2)}) %copy-start) | copy-done | bytes 2097176
  2.2 0.0 copy-start.1
  2.2 0.9 %copy-done.1 = bf16[2,48,512]{2,1,0:T(8,128)(2,1)S(1)} copy-done((bf16[2,48,512]{2,1,0:T(8,128)(2,1)S(1)}, bf16[2,48,512]{2,1,0:T(8,128)(2,1)}, u32[]{:S(2)}) %copy-start.1) | copy-done | bytes 98328
  3.1 0.0 copy-start.2
  3.1 0.0 copy-start.3
  3.1 46.4 %gather_factor.1 = (bf16[2,512,512]{2,1,0:T(8,128)(2,1)S(1)}, bf16[2,512,512]{2,1,0:T(8,128)(2,1)S(1)}, bf16[2,512,512]{2,1,0:T(8,128)(2,1)S(1)}, bf16[2,32,48,5...) custom-call(bf16[2,48,512]{2,1,0:T(8,128)(2,1)S(1)} %copy-done.1, f32[2,512,512]{2,1,0:T(8,128)S(1)} %copy-done), custom_call_target="tpu_custom_call" | custom-call | flops 10000000000 | bytes 10000000 | tf_op jit(solution)/shard_map/gather_factor/pallas_call | solution.py:323
  49.5 0.0 copy-start.4
  49.5 1.6 %copy-done.4 = bf16[2,32,48,512]{3,2,1,0:T(8,128)(2,1)} copy-done((bf16[2,32,48,512]{3,2,1,0:T(8,128)(2,1)}, bf16[2,32,48,512]{3,2,1,0:T(8,128)(2,1)S(1)}, u32[]{:S(2)}) %copy-start.4) | copy-done | bytes 3145752
  51.2 0.0 copy-done.2
  51.2 0.0 copy-done.3
  51.2 12.9 %solve_update.1 = (f32[2,384,1536]{2,1,0:T(8,128)}, f32[2,48,512]{2,1,0:T(8,128)}) custom-call(s32[96]{0:T(128)S(1)} %copy-done.3, bf16[2,48,512]{2,1,0:T(8,128)(2,1)S(1)} %copy-done.2, bf16[2,384,512]{2,1,0:T(8,128)(2,1)S(1)} %bitcast.3, bf16[2,1536,512]{2,1,0:T(8,128)(2,1)} %bitcast.2, bf16[2,512,512]{2,1,0:T(8,128)(2,1)S(1)} %get-tuple-element.9.hi_ref, ...), custom_call_target="tpu_custom_call" | custom-call | flops 6000000000 | bytes 16000000 | tf_op jit(solution)/shard_map/solve_update/pallas_call | solution.py:401
Async XLA Ops:
  0.6 1.6 %copy-start = (f32[2,512,512]{2,1,0:T(8,128)S(1)}, f32[2,512,512]{2,1,0:T(8,128)}, u32[]{:S(2)}) copy-start(f32[2,512,512]{2,1,0:T(8,128)} %diag.1) | copy-start | bytes 6291460
  2.2 0.9 %copy-start.1 = (bf16[2,48,512]{2,1,0:T(8,128)(2,1)S(1)}, bf16[2,48,512]{2,1,0:T(8,128)(2,1)}, u32[]{:S(2)}) copy-start(bf16[2,48,512]{2,1,0:T(8,128)(2,1)} %own_ref.1) | copy-start | bytes 294916
  3.1 48.1 %copy-start.2 = (bf16[2,48,512]{2,1,0:T(8,128)(2,1)S(1)}, bf16[2,48,512]{2,1,0:T(8,128)(2,1)}, u32[]{:S(2)}) copy-start(bf16[2,48,512]{2,1,0:T(8,128)(2,1)} %own_ref.1) | copy-start | bytes 294916
  3.1 48.1 %copy-start.3 = (s32[96]{0:T(128)S(1)}, s32[96]{0:T(128)}, u32[]{:S(2)}) copy-start(s32[96]{0:T(128)} %pat_ref.1) | copy-start | bytes 1156
  49.5 1.7 %copy-start.4 = (bf16[2,32,48,512]{3,2,1,0:T(8,128)(2,1)}, bf16[2,32,48,512]{3,2,1,0:T(8,128)(2,1)S(1)}, u32[]{:S(2)}) copy-start(bf16[2,32,48,512]{3,2,1,0:T(8,128)(2,1)S(1)} %get-tuple-element.8) | copy-start | bytes 9437188

commit v3 on v2

--- a/solution.py
+++ b/solution.py
@@ -38,6 +38,7 @@
     63: [('B', 1, 3), ('B', 1, -3)],
     64: [('B', 2, 2), ('B', 2, -2), ('B', -1, 4), ('B', 1, 4), ('B', 2, 3), ('B', 2, -3), ('B', 2, 4)],
 }
+LAST = 64
 PART = {"A": (0, 16), "B": (16, 32)}
 
 
@@ -242,9 +243,7 @@
     return jnp.concatenate(out, axis=0)
 
 
-def factor(diag_ref, w, v, s6, point):
-    for b in range(2):
-        w[b] = diag_ref[b]
+def factor(w, v, s6, point):
     lane = lax.broadcasted_iota(jnp.int32, (8, 128), 1)
     wide = lax.broadcasted_iota(jnp.int32, (64, 512), 1)
     wide2 = lax.broadcasted_iota(jnp.int32, (128, 512), 1)
@@ -297,10 +296,27 @@
     lax.fori_loop(0, 4, step, 0)
 
 
-def gather_factor_kernel(panel, diag, hi, mid, lo, cols, rows, w, v, s6, *sems):
+def solve(x, ys, b):
+    half = x.shape[1] // 2
+    out = []
+    for lo, depth in ((0, half), (half, 2 * half)):
+        acc = None
+        for y in ys:
+            term = dot(x[:, :depth], y[b, lo : lo + half, :depth], 1, 1)
+            acc = term if acc is None else acc + term
+        out.append(acc)
+    return jnp.concatenate(out, axis=1)
+
+
+def panel_kernel(panel, diag, trail, cols_out, rows_out, own_out, trail_out, cols, rows, w, v, s6, hi, mid, lo, full, in_sems, *sems):
+    fetch = pltpu.make_async_copy(diag, w, in_sems.at[0])
+    fetch.start()
     gather = Gather(panel, cols, rows, *sems)
     gather.barrier()
     gather.start()
+    fetch_trail = pltpu.make_async_copy(trail, trail_out, in_sems.at[1])
+    fetch_trail.start()
+    fetch.wait()
 
     def point(t, s, p):
         for i in range(4):
@@ -308,128 +324,139 @@
             if h in PLAN:
                 pl.when(t == i)(functools.partial(gather.point, h))
 
-    factor(diag, w, v, s6, point)
+    factor(w, v, s6, point)
+    ys = (hi, mid, lo)
     for b in range(2):
         hi[b], mid[b], lo[b] = split3(w[b])
-    gather.point(64)
-    gather.wait_rows()
+
+    def solve_cols(group):
+        slots = [gather.slot(dx, dz) for dx, dz in group]
+        for b in range(2):
+            x = jnp.concatenate([cols[b, i] for i in slots], axis=0)
+            x = solve(x, ys, b).astype(BF)
+            for n, i in enumerate(slots):
+                cols_out[b, i] = x[48 * n : 48 * n + 48]
+
+    def solve_rows():
+        gather.wait_rows()
+        for b in range(2):
+            full[b] = solve(jnp.concatenate([rows[b, i] for i in range(NC)], axis=0), ys, b)
+            for i in range(NC):
+                rows_out[b, i] = full[b, 48 * i : 48 * i + 48].astype(BF)
+            own_out[b] = full[b, pl.ds(pl.multiple_of(gather.col * 48, 16), 48)]
+
+    done = [e for h in sorted(PLAN) if h < LAST for e in PLAN[h]]
+    late = list(PLAN[LAST])
+    ready = [e[1:] for e in done if ("A",) + e[1:] in done and e[0] == "B"]
+    solve_rows()
+    while late or ready:
+        while late and (len(ready) < 4 or len(late) > 3 * len(ready)):
+            event = late.pop(0)
+            gather.arrival(*event)
+            done.append(event)
+            if ("A",) + event[1:] in done and ("B",) + event[1:] in done:
+                ready.append(event[1:])
+        solve_cols(ready[:4])
+        ready = ready[4:]
     gather.drain()
-
-
-def gather_factor(panel, diagonal):
+    fetch_trail.wait()
+
+
+def panel_step(panel, diagonal, trailing):
     nb, count, k = panel.shape
     vmem = pl.BlockSpec(memory_space=pltpu.VMEM)
-    y = jax.ShapeDtypeStruct(diagonal.shape, BF)
+    hbm = pl.BlockSpec(memory_space=pltpu.HBM)
     return pl.pallas_call(
-        gather_factor_kernel,
-        in_specs=[vmem] * 2,
-        out_specs=[vmem] * 5,
+        panel_kernel,
+        in_specs=[hbm] * 3,
+        out_specs=[vmem] * 4,
         out_shape=[
-            y, y, y,
             jax.ShapeDtypeStruct((nb, NX * NZ, count, k), BF),
             jax.ShapeDtypeStruct((nb, NC, count, k), BF),
+            jax.ShapeDtypeStruct(panel.shape, F32),
+            jax.ShapeDtypeStruct(trailing.shape, F32),
         ],
         scratch_shapes=[
+            pltpu.VMEM((nb, NX * NZ, count, k), BF),
+            pltpu.VMEM((nb, NC, count, k), BF),
             pltpu.VMEM(diagonal.shape, F32),
-            pltpu.VMEM((2, 128, 512), F32),
-            pltpu.VMEM((2, 768, 512), BF),
+            pltpu.VMEM((nb, 128, k), F32),
+            pltpu.VMEM((nb, 768, k), BF),
+            pltpu.VMEM(diagonal.shape, BF),
+            pltpu.VMEM(diagonal.shape, BF),
+            pltpu.VMEM(diagonal.shape, BF),
+            pltpu.VMEM((nb, NC * count, k), F32),
+            DMA((2,)),
         ] + GATHER_SEMS,
         compiler_params=pltpu.CompilerParams(
-            collective_id=0, has_side_effects=True, vmem_limit_bytes=40 << 20
+            collective_id=0, has_side_effects=True, vmem_limit_bytes=42 << 20
         ),
         cost_estimate=pl.CostEstimate(flops=10**10, bytes_accessed=10**7, transcendentals=0),
-        name="gather_factor",
-    )(panel, diagonal)
-
-
-def solve_rows(p, y_refs, b):
-    half = p.shape[1] // 2
-    parts = []
-    for lo, depth in ((0, half), (half, 2 * half)):
-        acc = None
-        for y in y_refs:
-            term = lax.dot_general(
-                p[:, :depth],
-                y[b, lo : lo + half, :depth],
-                (((1,), (1,)), ((), ())),
-                preferred_element_type=F32,
-            )
-            acc = term if acc is None else acc + term
-        parts.append(acc)
-    return jnp.concatenate(parts, axis=1)
-
-
-def keep_rows(x, pat_ref, first_block):
-    blocks = [
-        x[i * BLK : (i + 1) * BLK] * pat_ref[first_block + i].astype(F32)
-        for i in range(x.shape[0] // BLK)
-    ]
-    return jnp.concatenate(blocks, axis=0)
-
-
-def update_kernel(pat_ref, own_ref, row_ref, col_ref, hi_ref, mid_ref, lo_ref, trail_ref, out_ref, solved_ref, rows):
-    b = pl.program_id(0)
-    tile = pl.program_id(1)
+        name="panel_step",
+    )(*(pltpu.with_memory_space_constraint(a, pltpu.HBM) for a in (panel, diagonal, trailing)))
+
+
+WIDE = 256
+
+
+def update_kernel(pat, cols, rows, own, trail, out, solved, buf, own_buf, sems, own_sem):
     row, col = lax.axis_index("row"), lax.axis_index("col")
-    ys = (hi_ref, mid_ref, lo_ref)
-
-    @pl.when(tile == 0)
-    def _():
-        r = solve_rows(row_ref[0], ys, b)
-        rows[...] = keep_rows(r, pat_ref, row * 3).astype(jnp.bfloat16)
-        own = solve_rows(own_ref[0], ys, b)
-        first = (row * 8 + col) * 48
-        low = first // BLK
-        high = (first + 47) // BLK
-        at = first + lax.broadcasted_iota(jnp.int32, own.shape, 0)
-        keep = jnp.where(at < high * BLK, pat_ref[low], pat_ref[high]).astype(F32)
-        solved_ref[0] = own * keep
-
-    c = solve_rows(col_ref[0], ys, b)
-    per = col_ref.shape[1] // BLK
-    c = keep_rows(c, pat_ref, col * 12 + tile * per).astype(jnp.bfloat16)
-    out_ref[0] = trail_ref[0] - lax.dot_general(
-        rows[...], c, (((1,), (1,)), ((), ())), preferred_element_type=F32
-    )
-
-
-def update(pattern, own, rowp, colp, ys, trailing):
+    nb, m, n = buf.shape
+    count = own.shape[1]
+    first = (row * NC + col) * count
+    low, high = first // BLK, (first + count - 1) // BLK
+    at = first + lax.broadcasted_iota(jnp.int32, own.shape[1:], 0)
+    keep = jnp.where(at < high * BLK, pat[low], pat[high]).astype(F32)
+    for b in range(nb):
+        own_buf[b] = own[b] * keep
+    own_copy = pltpu.make_async_copy(own_buf, solved, own_sem)
+    own_copy.start()
+    keep_rows = [pat[row * (m // BLK) + i] for i in range(m // BLK)]
+    copies = []
+    for b in range(nb):
+        for j in range(n // WIDE):
+            there = pl.ds(j * WIDE, WIDE)
+            prod = dot(rows[b], cols[b, there], 1, 1)
+            for q in range(WIDE // BLK):
+                keep_col = pat[col * (n // BLK) + j * (WIDE // BLK) + q]
+                for i, keep_row in enumerate(keep_rows):
+                    r = slice(i * BLK, (i + 1) * BLK)
+                    c = slice(j * WIDE + q * BLK, j * WIDE + (q + 1) * BLK)
+                    both = (keep_col * keep_row).astype(F32)
+                    buf[b, r, c] = trail[b, r, c] - both * prod[r, q * BLK : (q + 1) * BLK]
+            copy = pltpu.make_async_copy(buf.at[b, :, there], out.at[b, :, there], sems.at[b, j])
+            copy.start()
+            copies.append(copy)
+    for copy in copies:
+        copy.wait()
+    own_copy.wait()
+
+
+def update(pattern, cols, rows, own, trailing):
+    vmem = pl.BlockSpec(memory_space=pltpu.VMEM)
+    hbm = pl.BlockSpec(memory_space=pltpu.HBM)
     nb, m, n = trailing.shape
-    width = 512
-    k = own.shape[2]
-    whole = pl.BlockSpec((nb, k, k), lambda b, t: (0, 0, 0))
     return pl.pallas_call(
         update_kernel,
-        grid=(nb, n // width),
-        in_specs=[
-            pl.BlockSpec(memory_space=pltpu.SMEM),
-            pl.BlockSpec((1, own.shape[1], k), lambda b, t: (b, 0, 0)),
-            pl.BlockSpec((1, m, k), lambda b, t: (b, 0, 0)),
-            pl.BlockSpec((1, width, k), lambda b, t: (b, t, 0)),
-            whole,
-            whole,
-            whole,
-            pl.BlockSpec((1, m, width), lambda b, t: (b, 0, t)),
+        in_specs=[pl.BlockSpec(memory_space=pltpu.SMEM)] + [vmem] * 4,
+        out_specs=[hbm] * 2,
+        out_shape=[jax.ShapeDtypeStruct(trailing.shape, F32), jax.ShapeDtypeStruct(own.shape, F32)],
+        scratch_shapes=[
+            pltpu.VMEM(trailing.shape, F32),
+            pltpu.VMEM(own.shape, F32),
+            DMA((nb, n // WIDE)),
+            DMA,
         ],
-        out_specs=[
-            pl.BlockSpec((1, m, width), lambda b, t: (b, 0, t)),
-            pl.BlockSpec((1, own.shape[1], k), lambda b, t: (b, 0, 0)),
-        ],
-        out_shape=[
-            jax.ShapeDtypeStruct(trailing.shape, F32),
-            jax.ShapeDtypeStruct(own.shape, F32),
-        ],
-        scratch_shapes=[pltpu.VMEM((m, k), jnp.bfloat16)],
-        compiler_params=pltpu.CompilerParams(vmem_limit_bytes=48 << 20),
-        cost_estimate=pl.CostEstimate(flops=6 * 10**9, bytes_accessed=16 * 10**6, transcendentals=0),
-        name="solve_update",
-    )(pattern, own, rowp, colp, *ys, trailing)
+        compiler_params=pltpu.CompilerParams(vmem_limit_bytes=36 << 20),
+        cost_estimate=pl.CostEstimate(flops=10**9, bytes_accessed=10**7, transcendentals=0),
+        name="update",
+    )(pattern, cols, rows, own, trailing)
 
 
 def per_device(trailing, panel, diagonal, pattern):
-    hi, mid, lo, cols, rows = gather_factor(panel, diagonal)
+    cols, rows, own, trail = panel_step(panel, diagonal, trailing)
     nb, _, _, k = cols.shape
-    return tuple(update(pattern, panel, rows.reshape(nb, -1, k), cols.reshape(nb, -1, k), (hi, mid, lo), trailing))
+    return tuple(update(pattern, cols.reshape(nb, -1, k), rows.reshape(nb, -1, k), own, trail))
 
 
 def solution(mesh):

time: 64.4 us -> 58.2 us (0.904)
  local copies, waits for them, and re-layouts: 4.13 us -> 0.01 us
  Pallas kernels: 59.3 us -> 57.4 us
    unnamed x10 -> x2, local copies, waits for them, and re-layouts: 4.13 us -> 0.01 us
    pallas_call x2, Pallas kernels: 59.3 us -> 57.4 us  [the longest x1 53.9 us: panel_step(): pl.pallas_call(panel_kernel, in_specs=[hbm] * 3, out_specs=[vmem] * 4, ou...]
where the time goes in v3:
time: 58.2 us; the launch traced here: 58.1 us
  Pallas kernels  57.4 us (99%)
  between operations  0.65 us (1%)
    pallas_call x1, Pallas kernels, panel_step(): pl.pallas_call(panel_kernel, in_specs=[hbm] * 3, out_specs=[vmem] * 4, ou...  53.9 us
    pallas_call x1, Pallas kernels, update(): pl.pallas_call(update_kernel, in_specs=[pl.BlockSpec(memory_space=pltpu.S...  3.5 us

profile of v3, /device:TPU:2, one launch (start us, length us, event | category | flops | bytes accessed | tf_op | source)
XLA Modules:
  0.0 58.1 jit_solution(14514483733332878233)
XLA Ops:
  0.6 0.0 copy-start
  0.6 53.9 %panel_step.1 = (bf16[2,32,48,512]{3,2,1,0:T(8,128)(2,1)S(1)}, bf16[2,8,48,512]{3,2,1,0:T(8,128)(2,1)S(1)}, f32[2,48,512]{2,1,0:T(8,128)S(1)}, f32[2,384,1536]{2,1,0:T(8,128)S(1)}) custom-call(bf16[2,48,512]{2,1,0:T(8,128)(2,1)} %panel.1, f32[2,512,512]{2,1,0:T(8,128)} %diag.1, f32[2,384,1536]{2,1,0:T(8,128)} %trail.1), custom_call_target="tpu_custom_call" | custom-call | flops 10000000000 | bytes 10000000 | tf_op jit(solution)/shard_map/panel_step/pallas_call | solution.py:369
  54.6 0.0 copy-done
  54.6 3.5 %update.1 = (f32[2,384,1536]{2,1,0:T(8,128)}, f32[2,48,512]{2,1,0:T(8,128)}) custom-call(s32[96]{0:T(128)S(1)} %copy-done, bf16[2,1536,512]{2,1,0:T(8,128)(2,1)S(1)} %bitcast.2, bf16[2,384,512]{2,1,0:T(8,128)(2,1)S(1)} %bitcast.3, f32[2,48,512]{2,1,0:T(8,128)S(1)} %get-tuple-element.8.own, f32[2,384,1536]{2,1,0:T(8,128)S(1)} %get-tuple-element.9.trail), custom_call_target="tpu_custom_call" | custom-call | flops 1000000000 | bytes 10000000 | tf_op jit(solution)/shard_map/update/pallas_call | solution.py:439
Async XLA Ops:
  0.6 54.0 %copy-start = (s32[96]{0:T(128)S(1)}, s32[96]{0:T(128)}, u32[]{:S(2)}) copy-start(s32[96]{0:T(128)} %pat.1) | copy-start | bytes 1156

commit v4 on v3

--- a/solution.py
+++ b/solution.py
@@ -15,28 +15,31 @@
 NX, NZ, NC = 4, 8, 8
 
 PLAN = {
-    11: [('A', 0, 0), ('B', 0, 0)],
-    19: [('A', 1, 0), ('A', -1, 0), ('A', 0, 1), ('A', 0, -1)],
-    21: [('B', 1, 0), ('B', -1, 0), ('B', 0, 1), ('B', 0, -1)],
-    25: [('A', 2, 0)],
-    30: [('A', 1, 1), ('A', -1, 1), ('A', 0, 2), ('A', 1, -1), ('A', -1, -1), ('A', 0, -2)],
-    33: [('B', -1, 1), ('B', -1, -1), ('A', 2, 1), ('A', 2, -1)],
-    34: [('B', 0, 2), ('B', 0, -2)],
-    36: [('B', 2, 0), ('B', 1, 1), ('B', 1, -1)],
-    41: [('A', 1, 2), ('A', -1, 2), ('A', 0, 3), ('A', 1, -2), ('A', -1, -2), ('A', 0, -3)],
-    43: [('A', 2, 2), ('A', 2, -2)],
-    45: [('B', 0, 3), ('B', 0, -3)],
-    46: [('B', 1, 2), ('B', 1, -2)],
-    50: [('A', 1, -3), ('A', -1, -3)],
-    51: [('A', 2, -3), ('B', 2, 1), ('B', 2, -1)],
-    53: [('A', 1, 3), ('A', -1, 3), ('A', 0, 4), ('B', -1, 2), ('B', -1, -2)],
-    54: [('A', 2, 3)],
-    56: [('B', 0, 4)],
-    57: [('A', -1, 4)],
-    58: [('A', 2, 4)],
-    59: [('B', -1, 3), ('B', -1, -3), ('A', 1, 4)],
-    63: [('B', 1, 3), ('B', 1, -3)],
-    64: [('B', 2, 2), ('B', 2, -2), ('B', -1, 4), ('B', 1, 4), ('B', 2, 3), ('B', 2, -3), ('B', 2, 4)],
+    5: [('A', 0, 0), ('B', 0, 0)],
+    13: [('A', 1, 0), ('A', -1, 0), ('A', 0, 1), ('A', 0, -1)],
+    15: [('B', 1, 0), ('B', -1, 0), ('B', 0, 1), ('B', 0, -1)],
+    19: [('A', 2, 0)],
+    24: [('A', 1, 1), ('A', -1, 1), ('A', 0, 2), ('A', 1, -1), ('A', -1, -1), ('A', 0, -2)],
+    27: [('B', -1, 1), ('B', -1, -1)],
+    28: [('A', 2, 1), ('A', 2, -1)],
+    29: [('B', 0, 2), ('B', 0, -2)],
+    31: [('B', 2, 0), ('B', 1, 1), ('B', 1, -1)],
+    35: [('A', 1, 2), ('A', -1, 2), ('A', 0, 3), ('A', 1, -2), ('A', -1, -2), ('A', 0, -3)],
+    38: [('A', 2, 2), ('A', 2, -2)],
+    40: [('B', 0, 3), ('B', 0, -3)],
+    41: [('B', 1, 2), ('B', 1, -2)],
+    44: [('A', 1, -3), ('A', -1, -3), ('B', 2, 1), ('B', 2, -1)],
+    45: [('A', 2, -3)],
+    46: [('A', 1, 3), ('A', -1, 3), ('A', 0, 4)],
+    48: [('B', -1, 2), ('B', -1, -2), ('A', 2, 3)],
+    51: [('B', 0, 4), ('A', -1, 4)],
+    52: [('A', 2, 4), ('A', 1, 4)],
+    54: [('B', -1, 3), ('B', -1, -3)],
+    59: [('B', 1, 3), ('B', 1, -3)],
+    60: [('B', 2, 2), ('B', 2, -2)],
+    61: [('B', -1, 4)],
+    63: [('B', 1, 4)],
+    64: [('B', 2, 3), ('B', 2, -3), ('B', 2, 4)],
 }
 LAST = 64
 PART = {"A": (0, 16), "B": (16, 32)}
@@ -247,53 +250,58 @@
     lane = lax.broadcasted_iota(jnp.int32, (8, 128), 1)
     wide = lax.broadcasted_iota(jnp.int32, (64, 512), 1)
     wide2 = lax.broadcasted_iota(jnp.int32, (128, 512), 1)
-
-    def step(t, carry):
-        o = pl.multiple_of(t * 128, 128)
+    band = lax.broadcasted_iota(jnp.int32, (128, 128), 0) // 64
+    same = band == lax.broadcasted_iota(jnp.int32, (128, 128), 1) // 64
+
+    for t in range(4):
+        o = t * 128
         for s in range(2):
-            at = pl.multiple_of(o + 64 * s, 64)
+            at = o + 64 * s
             x = []
             for g in range(8):
-                rows = pl.ds(pl.multiple_of(at + 8 * g, 8), 8)
+                rows = pl.ds(at + 8 * g, 8)
                 a, b = w[0, rows, pl.ds(o, 128)], w[1, rows, pl.ds(o, 128)]
                 if s == 0:
                     x.append(jnp.where(lane < 64, a, pltpu.roll(b, 64, 1)))
                 else:
                     x.append(jnp.where(lane < 64, pltpu.roll(a, 64, 1), b))
             y = base(x, functools.partial(point, t, s))
-            here = (wide >= at) & (wide < at + 64)
+            both = jnp.concatenate([w[0, pl.ds(at, 64), :], w[1, pl.ds(at, 64), :]], axis=0)
+            ys = jnp.where(same, jnp.concatenate([y, y], axis=0), 0.0)
+            new = dot(stack6(ys, 1, True), stack6(both, 0, False), 1, 0)
+            here = (wide2 >= at) & (wide2 < at + 64)
+            yt = jnp.where(same, ys, pltpu.roll(ys, 64, 1))
+            yt = jnp.concatenate([yt] * 4, axis=1)
+            new = jnp.where(here, yt, new)
             for b in range(2):
-                yb = y[:, 64 * b : 64 * b + 64]
-                new = dot(yb, w[b, pl.ds(at, 64), :], 1, 0, HIGHEST)
-                new = jnp.where(here, jnp.concatenate([yb] * 8, axis=1), new)
-                w[b, pl.ds(at, 64), :] = jnp.where(wide < at + 64, new, 0.0)
+                part = new[64 * b : 64 * b + 64]
+                w[b, pl.ds(at, 64), :] = jnp.where(wide < at + 64, part, 0.0)
                 if s == 0:
-                    v[b, 0:64, :] = jnp.where((wide >= at + 64) & (wide < at + 128), 0.0, new)
-                    below = w[b, pl.ds(at + 64, 64), pl.ds(o, 128)][:, 0:64]
-                    lower = dot(below, yb, 1, 1, HIGHEST)
-                    rest = jnp.where(here, 0.0, w[b, pl.ds(at + 64, 64), :])
-                    w[b, pl.ds(at + 64, 64), :] = rest - dot(lower, new, 1, 0, HIGHEST)
-                else:
-                    v[b, 64:128, :] = new
+                    part = jnp.where((wide >= at + 64) & (wide < at + 128), 0.0, part)
+                v[b, 64 * s : 64 * s + 64, :] = part
+            if s == 0:
+                below = [w[b, pl.ds(at + 64, 64), pl.ds(o, 128)] for b in range(2)]
+                below = jnp.concatenate([below[0], pltpu.roll(below[1], 64, 1)], axis=0)
+                below = jnp.where(same, below, 0.0)
+                lower = dot(stack6(below, 1, True), stack6(jnp.concatenate([y, y], axis=0), 1, False), 1, 1)
+                lower = jnp.where(same, lower, 0.0)
+                rest = [w[b, pl.ds(at + 64, 64), :] for b in range(2)]
+                rest = jnp.where(here, 0.0, jnp.concatenate(rest, axis=0))
+                rest = rest - dot(stack6(lower, 1, True), stack6(new, 0, False), 1, 0)
+                for b in range(2):
+                    w[b, pl.ds(at + 64, 64), :] = rest[64 * b : 64 * b + 64]
         here = (wide2 >= o) & (wide2 < o + 128)
 
-        @pl.when(t < 3)
-        def _():
+        if t < 3:
             for b in range(2):
                 s6[b] = stack6(v[b], 0, False)
 
-        def chunk(i, c):
-            rows = pl.ds(pl.multiple_of(i * 128, 128), 128)
+        for i in range(t + 1, 4):
+            rows = pl.ds(i * 128, 128)
             for b in range(2):
                 lower = v[b, :, rows].T
                 rest = jnp.where(here, 0.0, w[b, rows, :])
                 w[b, rows, :] = rest - dot(stack6(lower, 1, True), s6[b], 1, 0)
-            return c
-
-        lax.fori_loop(t + 1, 4, chunk, 0)
-        return carry
-
-    lax.fori_loop(0, 4, step, 0)
 
 
 def solve(x, ys, b):
@@ -319,10 +327,7 @@
     fetch.wait()
 
     def point(t, s, p):
-        for i in range(4):
-            h = (2 * i + s) * 8 + p
-            if h in PLAN:
-                pl.when(t == i)(functools.partial(gather.point, h))
+        gather.point((2 * t + s) * 8 + p)
 
     factor(w, v, s6, point)
     ys = (hi, mid, lo)

time: 58.2 us -> 55.7 us (0.957)
  Pallas kernels: 57.4 us -> 54.7 us
    pallas_call x1, Pallas kernels: 53.9 us -> 51.2 us  [panel_step(): pl.pallas_call(panel_kernel, in_specs=[hbm] * 3, out_specs=[vmem] * 4, ou...]
where the time goes in v4:
time: 55.7 us; the launch traced here: 55.6 us
  Pallas kernels  54.7 us (98%)
  between operations  0.81 us (1%)
    pallas_call x1, Pallas kernels, panel_step(): pl.pallas_call(panel_kernel, in_specs=[hbm] * 3, out_specs=[vmem] * 4, ou...  51.2 us
    pallas_call x1, Pallas kernels, update(): pl.pallas_call(update_kernel, in_specs=[pl.BlockSpec(memory_space=pltpu.S...  3.51 us

profile of v4, /device:TPU:2, one launch (start us, length us, event | category | flops | bytes accessed | tf_op | source)
XLA Modules:
  0.0 55.6 jit_solution(10862291666214613762)
XLA Ops:
  0.6 0.0 copy-start
  0.6 51.2 %panel_step.1 = (bf16[2,32,48,512]{3,2,1,0:T(8,128)(2,1)S(1)}, bf16[2,8,48,512]{3,2,1,0:T(8,128)(2,1)S(1)}, f32[2,48,512]{2,1,0:T(8,128)S(1)}, f32[2,384,1536]{2,1,0:T(8,128)S(1)}) custom-call(bf16[2,48,512]{2,1,0:T(8,128)(2,1)} %panel.1, f32[2,512,512]{2,1,0:T(8,128)} %diag.1, f32[2,384,1536]{2,1,0:T(8,128)} %trail.1), custom_call_target="tpu_custom_call" | custom-call | flops 10000000000 | bytes 10000000 | tf_op jit(solution)/shard_map/panel_step/pallas_call | solution.py:374
  51.9 0.0 copy-done
  51.9 3.5 %update.1 = (f32[2,384,1536]{2,1,0:T(8,128)}, f32[2,48,512]{2,1,0:T(8,128)}) custom-call(s32[96]{0:T(128)S(1)} %copy-done, bf16[2,1536,512]{2,1,0:T(8,128)(2,1)S(1)} %bitcast.2, bf16[2,384,512]{2,1,0:T(8,128)(2,1)S(1)} %bitcast.3, f32[2,48,512]{2,1,0:T(8,128)S(1)} %get-tuple-element.8.own, f32[2,384,1536]{2,1,0:T(8,128)S(1)} %get-tuple-element.9.trail), custom_call_target="tpu_custom_call" | custom-call | flops 1000000000 | bytes 10000000 | tf_op jit(solution)/shard_map/update/pallas_call | solution.py:444
Async XLA Ops:
  0.6 51.3 %copy-start = (s32[96]{0:T(128)S(1)}, s32[96]{0:T(128)}, u32[]{:S(2)}) copy-start(s32[96]{0:T(128)} %pat.1) | copy-start | bytes 1156

commit v5 on v4

--- a/solution.py
+++ b/solution.py
@@ -15,29 +15,30 @@
 NX, NZ, NC = 4, 8, 8
 
 PLAN = {
-    5: [('A', 0, 0), ('B', 0, 0)],
-    13: [('A', 1, 0), ('A', -1, 0), ('A', 0, 1), ('A', 0, -1)],
-    15: [('B', 1, 0), ('B', -1, 0), ('B', 0, 1), ('B', 0, -1)],
-    19: [('A', 2, 0)],
-    24: [('A', 1, 1), ('A', -1, 1), ('A', 0, 2), ('A', 1, -1), ('A', -1, -1), ('A', 0, -2)],
-    27: [('B', -1, 1), ('B', -1, -1)],
-    28: [('A', 2, 1), ('A', 2, -1)],
-    29: [('B', 0, 2), ('B', 0, -2)],
+    3: [('A', 0, 0)],
+    5: [('B', 0, 0)],
+    10: [('A', 1, 0), ('A', -1, 0), ('A', 0, 1), ('A', 0, -1)],
+    14: [('B', 1, 0), ('B', -1, 0), ('B', 0, 1), ('B', 0, -1)],
+    17: [('A', 2, 0)],
+    22: [('A', 1, 1), ('A', -1, 1), ('A', 0, 2), ('A', 1, -1), ('A', -1, -1), ('A', 0, -2)],
+    26: [('A', 2, 1), ('A', 2, -1)],
+    27: [('B', 0, 2), ('B', 0, -2), ('B', -1, 1), ('B', -1, -1)],
     31: [('B', 2, 0), ('B', 1, 1), ('B', 1, -1)],
-    35: [('A', 1, 2), ('A', -1, 2), ('A', 0, 3), ('A', 1, -2), ('A', -1, -2), ('A', 0, -3)],
-    38: [('A', 2, 2), ('A', 2, -2)],
-    40: [('B', 0, 3), ('B', 0, -3)],
-    41: [('B', 1, 2), ('B', 1, -2)],
-    44: [('A', 1, -3), ('A', -1, -3), ('B', 2, 1), ('B', 2, -1)],
+    34: [('A', 1, 2), ('A', -1, 2), ('A', 0, 3), ('A', 1, -2), ('A', -1, -2), ('A', 0, -3)],
+    37: [('A', 2, 2), ('A', 2, -2)],
+    39: [('B', 0, 3), ('B', 0, -3)],
+    40: [('B', 1, 2), ('B', 1, -2)],
+    44: [('A', 1, -3), ('A', -1, -3)],
     45: [('A', 2, -3)],
     46: [('A', 1, 3), ('A', -1, 3), ('A', 0, 4)],
-    48: [('B', -1, 2), ('B', -1, -2), ('A', 2, 3)],
-    51: [('B', 0, 4), ('A', -1, 4)],
-    52: [('A', 2, 4), ('A', 1, 4)],
-    54: [('B', -1, 3), ('B', -1, -3)],
+    48: [('A', 2, 3)],
+    49: [('B', -1, 2), ('B', -1, -2), ('B', 2, 1), ('B', 2, -1)],
+    51: [('B', 0, 4)],
+    52: [('A', -1, 4)],
+    53: [('A', 2, 4), ('A', 1, 4)],
+    55: [('B', -1, 3), ('B', -1, -3)],
     59: [('B', 1, 3), ('B', 1, -3)],
-    60: [('B', 2, 2), ('B', 2, -2)],
-    61: [('B', -1, 4)],
+    60: [('B', 2, 2), ('B', 2, -2), ('B', -1, 4)],
     63: [('B', 1, 4)],
     64: [('B', 2, 3), ('B', 2, -3), ('B', 2, 4)],
 }
@@ -119,14 +120,19 @@
 
         pl.when(self.stays)(lambda: pl.semaphore_wait(sem, len(near)))
 
-    def first(self, slot):
+    def first(self, part, slot):
+        i = 0 if part == "A" else 1
         return pltpu.make_async_remote_copy(
-            self.panel, self.cols.at[:, slot], self.first_sem, self.arrive_sem,
+            self.panel.at[:, pl.ds(*PART[part])], self.piece(part, slot),
+            self.first_sem.at[i], self.arrive_sem.at[i],
             device_id=(self.to_row, self.to_col), device_id_type=MESH,
         )
 
-    def first_stays(self):
-        return pltpu.make_async_copy(self.panel, self.cols.at[:, self.home], self.first_sem)
+    def first_stays(self, part):
+        return pltpu.make_async_copy(
+            self.panel.at[:, pl.ds(*PART[part])], self.piece(part, self.home),
+            self.first_sem.at[0 if part == "A" else 1],
+        )
 
     def row_copy(self, i, col):
         return pltpu.make_async_remote_copy(
@@ -138,8 +144,9 @@
         return pltpu.make_async_copy(self.panel, self.rows.at[:, self.col], self.own_sem)
 
     def start(self):
-        pl.when(self.moves)(lambda: self.first(self.to_slot).start())
-        pl.when(self.stays)(lambda: self.first_stays().start())
+        for part in PART:
+            pl.when(self.moves)(lambda: self.first(part, self.to_slot).start())
+            pl.when(self.stays)(lambda: self.first_stays(part).start())
         for i in range(NC - 1):
             self.row_copy(i, self.col).start()
         self.row_own().start()
@@ -158,9 +165,9 @@
         slot = self.slot(dx, dz)
         if (dx, dz) != (0, 0):
             self.move(part, slot, 0, dx, dz, self.neighbour("x", 1)).wait_recv()
-        elif part == "A":
-            pl.when(self.moves)(lambda: self.first(self.home).wait_recv())
-            pl.when(self.stays)(lambda: self.first_stays().wait())
+        else:
+            pl.when(self.moves)(lambda: self.first(part, self.home).wait_recv())
+            pl.when(self.stays)(lambda: self.first_stays(part).wait())
         for axis, step, ndx, ndz in onward(part, dx, dz):
             self.move(part, slot, len(self.sent), ndx, ndz, self.neighbour(axis, step)).start()
             self.sent.append(part)
@@ -177,13 +184,14 @@
     def drain(self):
         for i, part in enumerate(self.sent):
             self.move(part, self.home, i, 0, 0, self.neighbour("x", 1)).wait_send()
-        pl.when(self.moves)(lambda: self.first(self.to_slot).wait_send())
+        for part in PART:
+            pl.when(self.moves)(lambda: self.first(part, self.to_slot).wait_send())
         for i in range(NC - 1):
             self.row_copy(i, self.col).wait_send()
 
 
 DMA = pltpu.SemaphoreType.DMA
-GATHER_SEMS = [DMA, DMA, DMA((62,)), DMA((2, NX * NZ)), DMA((NC - 1,)), DMA((NC - 1,)), DMA]
+GATHER_SEMS = [DMA((2,)), DMA((2,)), DMA((62,)), DMA((2, NX * NZ)), DMA((NC - 1,)), DMA((NC - 1,)), DMA]
 
 
 def dot(a, b, ca, cb, precision=None):
@@ -338,7 +346,7 @@
         slots = [gather.slot(dx, dz) for dx, dz in group]
         for b in range(2):
             x = jnp.concatenate([cols[b, i] for i in slots], axis=0)
-            x = solve(x, ys, b).astype(BF)
+            x = solve(x, ys[:2], b).astype(BF)
             for n, i in enumerate(slots):
                 cols_out[b, i] = x[48 * n : 48 * n + 48]
 
@@ -355,14 +363,14 @@
     ready = [e[1:] for e in done if ("A",) + e[1:] in done and e[0] == "B"]
     solve_rows()
     while late or ready:
-        while late and (len(ready) < 4 or len(late) > 3 * len(ready)):
+        while late and (len(ready) < 8 or len(late) > 3 * len(ready)):
             event = late.pop(0)
             gather.arrival(*event)
             done.append(event)
             if ("A",) + event[1:] in done and ("B",) + event[1:] in done:
                 ready.append(event[1:])
-        solve_cols(ready[:4])
-        ready = ready[4:]
+        solve_cols(ready[:8])
+        ready = ready[8:]
     gather.drain()
     fetch_trail.wait()
 
@@ -401,7 +409,7 @@
     )(*(pltpu.with_memory_space_constraint(a, pltpu.HBM) for a in (panel, diagonal, trailing)))
 
 
-WIDE = 256
+WIDE = 512
 
 
 def update_kernel(pat, cols, rows, own, trail, out, solved, buf, own_buf, sems, own_sem):

time: 55.7 us -> 51.4 us (0.923)
  Pallas kernels: 54.7 us -> 50.4 us
    pallas_call x1, Pallas kernels: 51.2 us -> 47.2 us  [panel_step(): pl.pallas_call(panel_kernel, in_specs=[hbm] * 3, out_specs=[vmem] * 4, ou...]
where the time goes in v5:
time: 51.4 us; the launch traced here: 51.3 us
  Pallas kernels  50.4 us (98%)
  between operations  0.81 us (2%)
    pallas_call x1, Pallas kernels, panel_step(): pl.pallas_call(panel_kernel, in_specs=[hbm] * 3, out_specs=[vmem] * 4, ou...  47.2 us
    pallas_call x1, Pallas kernels, update(): pl.pallas_call(update_kernel, in_specs=[pl.BlockSpec(memory_space=pltpu.S...  3.27 us

profile of v5, /device:TPU:2, one launch (start us, length us, event | category | flops | bytes accessed | tf_op | source)
XLA Modules:
  0.0 51.3 jit_solution(11359428721841415855)
XLA Ops:
  0.6 0.0 copy-start
  0.6 47.2 %panel_step.1 = (bf16[2,32,48,512]{3,2,1,0:T(8,128)(2,1)S(1)}, bf16[2,8,48,512]{3,2,1,0:T(8,128)(2,1)S(1)}, f32[2,48,512]{2,1,0:T(8,128)S(1)}, f32[2,384,1536]{2,1,0:T(8,128)S(1)}) custom-call(bf16[2,48,512]{2,1,0:T(8,128)(2,1)} %panel.1, f32[2,512,512]{2,1,0:T(8,128)} %diag.1, f32[2,384,1536]{2,1,0:T(8,128)} %trail.1), custom_call_target="tpu_custom_call" | custom-call | flops 10000000000 | bytes 10000000 | tf_op jit(solution)/shard_map/panel_step/pallas_call | solution.py:382
  47.8 0.0 copy-done
  47.8 3.3 %update.1 = (f32[2,384,1536]{2,1,0:T(8,128)}, f32[2,48,512]{2,1,0:T(8,128)}) custom-call(s32[96]{0:T(128)S(1)} %copy-done, bf16[2,1536,512]{2,1,0:T(8,128)(2,1)S(1)} %bitcast.2, bf16[2,384,512]{2,1,0:T(8,128)(2,1)S(1)} %bitcast.3, f32[2,48,512]{2,1,0:T(8,128)S(1)} %get-tuple-element.8.own, f32[2,384,1536]{2,1,0:T(8,128)S(1)} %get-tuple-element.9.trail), custom_call_target="tpu_custom_call" | custom-call | flops 1000000000 | bytes 10000000 | tf_op jit(solution)/shard_map/update/pallas_call | solution.py:452
Async XLA Ops:
  0.6 47.2 %copy-start = (s32[96]{0:T(128)S(1)}, s32[96]{0:T(128)}, u32[]{:S(2)}) copy-start(s32[96]{0:T(128)} %pat.1) | copy-start | bytes 1156

commit v6 on v5

--- a/solution.py
+++ b/solution.py
@@ -43,6 +43,7 @@
     64: [('B', 2, 3), ('B', 2, -3), ('B', 2, 4)],
 }
 LAST = 64
+ROWS_AT = 8
 PART = {"A": (0, 16), "B": (16, 32)}
 
 
@@ -89,26 +90,28 @@
         self.from_col = ((x + NX - y) % NX) * 2 + u % 2
         self.stays = (self.to_row == self.row) & (self.to_col == self.col)
         self.moves = jnp.logical_not(self.stays)
+        self.slot_x = [((x + 2 * NX - dx - y) % NX) * 2 for dx in range(NX)]
+        us = [(z + 10 + NZ - dz - 4 * k) % NZ for dz in range(NZ)]
+        self.slot_z = [(u // 2) * NC + u % 2 for u in us]
         self.home = self.slot(0, 0)
+        self.near = {}
+        for step in (1, -1):
+            self.near["x", step] = (((x + step + NX) % NX) * NZ + z, self.col)
+            self.near["z", step] = (x * NZ + (z + step + NZ) % NZ, self.col)
         self.sent = []
 
     def slot(self, dx, dz):
-        xh = (self.x - dx + 2 * NX) % NX
-        u = (self.z - dz + 2 * NZ + 10 - 4 * self.k) % NZ
-        return (u // 2) * NC + ((xh + NX - self.y) % NX) * 2 + u % 2
+        return self.slot_x[dx % NX] + self.slot_z[dz % NZ]
 
     def neighbour(self, axis, step):
-        if axis == "x":
-            return (((self.x + step + NX) % NX) * NZ + self.z, self.col)
-        return (self.x * NZ + (self.z + step + NZ) % NZ, self.col)
+        return self.near[axis, step]
 
     def peer(self, i):
         return (self.row, (self.col + i) % NC)
 
     def barrier(self):
         sem = pltpu.get_barrier_semaphore()
-        near = [self.neighbour(a, s) for a in "xz" for s in (1, -1)]
-        near += [self.peer(i) for i in range(1, NC)]
+        near = list(self.near.values()) + [self.peer(i) for i in range(1, NC)]
         for d in near:
             pl.semaphore_signal(sem, inc=1, device_id=d, device_id_type=MESH)
 
@@ -147,6 +150,8 @@
         for part in PART:
             pl.when(self.moves)(lambda: self.first(part, self.to_slot).start())
             pl.when(self.stays)(lambda: self.first_stays(part).start())
+
+    def start_rows(self):
         for i in range(NC - 1):
             self.row_copy(i, self.col).start()
         self.row_own().start()
@@ -173,6 +178,8 @@
             self.sent.append(part)
 
     def point(self, h):
+        if h == ROWS_AT:
+            self.start_rows()
         for part, dx, dz in PLAN.get(h, ()):
             self.arrival(part, dx, dz)
 
@@ -246,7 +253,10 @@
                 if g == p:
                     m = jnp.where(sub > k, m, 0.0)
                 for c in range(k + 1, 8):
-                    t[g][c] = t[g][c] - m * top[c]
+                    if g == p and c == k + 1:
+                        t[g][c] = t[g][c] - jnp.where(sub > k, t[g][k] * top[c], 0.0) * r
+                    else:
+                        t[g][c] = t[g][c] - m * top[c]
                 if p < 7:
                     x[g] = x[g] - m * px
                 e[g] = e[g] - m * pe
@@ -359,7 +369,7 @@
             own_out[b] = full[b, pl.ds(pl.multiple_of(gather.col * 48, 16), 48)]
 
     done = [e for h in sorted(PLAN) if h < LAST for e in PLAN[h]]
-    late = list(PLAN[LAST])
+    late = list(PLAN.get(LAST, ()))
     ready = [e[1:] for e in done if ("A",) + e[1:] in done and e[0] == "B"]
     solve_rows()
     while late or ready:

time: 51.4 us -> 50.8 us (0.988)
    pallas_call x1, Pallas kernels: 47.2 us -> 46.6 us  [panel_step(): pl.pallas_call(panel_kernel, in_specs=[hbm] * 3, out_specs=[vmem] * 4, ou...]
where the time goes in v6:
time: 50.8 us; the launch traced here: 50.7 us
  Pallas kernels  49.9 us (98%)
  between operations  0.81 us (2%)
    pallas_call x1, Pallas kernels, panel_step(): pl.pallas_call(panel_kernel, in_specs=[hbm] * 3, out_specs=[vmem] * 4, ou...  46.6 us
    pallas_call x1, Pallas kernels, update(): pl.pallas_call(update_kernel, in_specs=[pl.BlockSpec(memory_space=pltpu.S...  3.27 us

profile of v6, /device:TPU:2, one launch (start us, length us, event | category | flops | bytes accessed | tf_op | source)
XLA Modules:
  0.0 50.7 jit_solution(10437945016302720711)
XLA Ops:
  0.6 0.0 copy-start
  0.6 46.6 %panel_step.1 = (bf16[2,32,48,512]{3,2,1,0:T(8,128)(2,1)S(1)}, bf16[2,8,48,512]{3,2,1,0:T(8,128)(2,1)S(1)}, f32[2,48,512]{2,1,0:T(8,128)S(1)}, f32[2,384,1536]{2,1,0:T(8,128)S(1)}) custom-call(bf16[2,48,512]{2,1,0:T(8,128)(2,1)} %panel.1, f32[2,512,512]{2,1,0:T(8,128)} %diag.1, f32[2,384,1536]{2,1,0:T(8,128)} %trail.1), custom_call_target="tpu_custom_call" | custom-call | flops 10000000000 | bytes 10000000 | tf_op jit(solution)/shard_map/panel_step/pallas_call | solution.py:392
  47.3 0.0 copy-done
  47.3 3.3 %update.1 = (f32[2,384,1536]{2,1,0:T(8,128)}, f32[2,48,512]{2,1,0:T(8,128)}) custom-call(s32[96]{0:T(128)S(1)} %copy-done, bf16[2,1536,512]{2,1,0:T(8,128)(2,1)S(1)} %bitcast.2, bf16[2,384,512]{2,1,0:T(8,128)(2,1)S(1)} %bitcast.3, f32[2,48,512]{2,1,0:T(8,128)S(1)} %get-tuple-element.8.own, f32[2,384,1536]{2,1,0:T(8,128)S(1)} %get-tuple-element.9.trail), custom_call_target="tpu_custom_call" | custom-call | flops 1000000000 | bytes 10000000 | tf_op jit(solution)/shard_map/update/pallas_call | solution.py:462
Async XLA Ops:
  0.6 46.7 %copy-start = (s32[96]{0:T(128)S(1)}, s32[96]{0:T(128)}, u32[]{:S(2)}) copy-start(s32[96]{0:T(128)} %pat.1) | copy-start | bytes 1156

commit v7 on v6

--- a/solution.py
+++ b/solution.py
@@ -43,7 +43,7 @@
     64: [('B', 2, 3), ('B', 2, -3), ('B', 2, 4)],
 }
 LAST = 64
-ROWS_AT = 8
+ROWS_AT = 16
 PART = {"A": (0, 16), "B": (16, 32)}
 
 

time: 50.8 us -> 50.8 us (level)
  no operation moved by 1% of the time
where the time goes in v7:
time: 50.8 us; the launch traced here: 50.7 us
  Pallas kernels  49.9 us (98%)
  between operations  0.81 us (2%)
    pallas_call x1, Pallas kernels, panel_step(): pl.pallas_call(panel_kernel, in_specs=[hbm] * 3, out_specs=[vmem] * 4, ou...  46.6 us
    pallas_call x1, Pallas kernels, update(): pl.pallas_call(update_kernel, in_specs=[pl.BlockSpec(memory_space=pltpu.S...  3.26 us

profile of v7, /device:TPU:2, one launch (start us, length us, event | category | flops | bytes accessed | tf_op | source)
XLA Modules:
  0.0 50.7 jit_solution(2674597131707140664)
XLA Ops:
  0.6 0.0 copy-start
  0.6 46.6 %panel_step.1 = (bf16[2,32,48,512]{3,2,1,0:T(8,128)(2,1)S(1)}, bf16[2,8,48,512]{3,2,1,0:T(8,128)(2,1)S(1)}, f32[2,48,512]{2,1,0:T(8,128)S(1)}, f32[2,384,1536]{2,1,0:T(8,128)S(1)}) custom-call(bf16[2,48,512]{2,1,0:T(8,128)(2,1)} %panel.1, f32[2,512,512]{2,1,0:T(8,128)} %diag.1, f32[2,384,1536]{2,1,0:T(8,128)} %trail.1), custom_call_target="tpu_custom_call" | custom-call | flops 10000000000 | bytes 10000000 | tf_op jit(solution)/shard_map/panel_step/pallas_call | solution.py:392
  47.3 0.0 copy-done
  47.3 3.3 %update.1 = (f32[2,384,1536]{2,1,0:T(8,128)}, f32[2,48,512]{2,1,0:T(8,128)}) custom-call(s32[96]{0:T(128)S(1)} %copy-done, bf16[2,1536,512]{2,1,0:T(8,128)(2,1)S(1)} %bitcast.2, bf16[2,384,512]{2,1,0:T(8,128)(2,1)S(1)} %bitcast.3, f32[2,48,512]{2,1,0:T(8,128)S(1)} %get-tuple-element.8.own, f32[2,384,1536]{2,1,0:T(8,128)S(1)} %get-tuple-element.9.trail), custom_call_target="tpu_custom_call" | custom-call | flops 1000000000 | bytes 10000000 | tf_op jit(solution)/shard_map/update/pallas_call | solution.py:462
Async XLA Ops:
  0.6 46.7 %copy-start = (s32[96]{0:T(128)S(1)}, s32[96]{0:T(128)}, u32[]{:S(2)}) copy-start(s32[96]{0:T(128)} %pat.1) | copy-start | bytes 1156
